TPU v7x, 512 devices: a whole 4x4x16 slice. The times are simulated.
512 devices in a mesh: loop: 64 (over x_hi, z, core), pool: 8 (over x_lo, y).
Axes of the slice: x: 4 (x_hi: 2, x_lo: 2; x = x_hi * 2 + x_lo), y: 4, z: 16, core: 2. Of those that a mesh axis runs over, the one named last changes fastest.
Arguments:
- picture_embedding_raw: bfloat16 [65536, 1152], P(('loop', 'pool')), may hold values from -0.1796875 to 0.1796875
- caption_embedding_raw: bfloat16 [65536, 1152], P(('loop', 'pool')), may hold values from -0.1796875 to 0.1796875
- score_sharpness: float32 [1], replicated, may hold values from 8 to 12
- score_shift_term: float32 [1], replicated, may hold values from -6 to -4
Outputs:
- image_grad: float32 [65536, 1152], P(('loop', 'pool'))
- text_grad: float32 [65536, 1152], P(('loop', 'pool'))
All inputs are finite; a program needn't handle non-finite values.
Results may differ from a plain program's by a relative error of at most 0.0095.
Values may be sent and summed in bfloat16 or wider, within the bound.
A program may use at most 64 MiB of HBM per device.

v0:
```python
import jax
import jax.numpy as jnp
from jax import lax
from jax.sharding import PartitionSpec as P

STEPS = 4


epsilon_norm = 1e-06


def passed_along(value, axis, steps):
    count = lax.axis_size(axis)
    pairs = [(source, (source + steps) % count) for source in range(count)]
    return lax.ppermute(value, axis, pairs)


def normalize(values):
    wide = values.astype(jnp.float32)
    inverse = lax.rsqrt(jnp.sum(wide * wide, axis=-1, keepdims=True) + epsilon_norm)
    return (wide * inverse, inverse)


def normalizer_reverse_pass(unit_rows, inverse, grad_hat):
    inner = jnp.sum(unit_rows * grad_hat, axis=-1, keepdims=True)
    return inverse * (grad_hat - unit_rows * inner)


def shards(picture_embedding_raw, caption_embedding_raw, score_sharpness, score_shift_term):
    row_count = picture_embedding_raw.shape[0]
    smoothing_multiplier = score_sharpness[0]
    logit_offset_bias = score_shift_term[0]
    image_unit, image_inverse = normalize(picture_embedding_raw)
    text_unit, text_inverse = normalize(caption_embedding_raw)
    picture_direction = image_unit.astype(jnp.bfloat16)
    text_hat = text_unit.astype(jnp.bfloat16)
    pooled = lax.all_gather(picture_direction, "pool", axis=0, tiled=True)
    group_rows = pooled.shape[0]

    def score_block(text_tile_rows, label_sign):
        pair_logit_matrix = (
            smoothing_multiplier
            * jnp.einsum("id,jd->ij", pooled, text_tile_rows, preferred_element_type=jnp.float32)
            + logit_offset_bias
        )
        weight_brain_float = (
            (jax.nn.sigmoid(pair_logit_matrix) - label_sign) * smoothing_multiplier
        ).astype(jnp.bfloat16)
        image_part = jnp.dot(weight_brain_float, text_tile_rows, preferred_element_type=jnp.float32)
        text_part = jnp.einsum(
            "ij,id->jd", weight_brain_float, pooled, preferred_element_type=jnp.float32
        )
        return (image_part, text_part)

    pool_index = lax.axis_index("pool")
    own_target = (
        jnp.arange(group_rows, dtype=jnp.int32)[:, None]
        == pool_index * row_count + jnp.arange(row_count, dtype=jnp.int32)[None, :]
    ).astype(jnp.float32)
    image_acc, text_acc = score_block(text_hat, own_target)
    ahead_text = text_hat
    behind_text = text_hat
    for offset in range(1, STEPS):
        ahead_text = passed_along(ahead_text, "loop", -1)
        behind_text = passed_along(behind_text, "loop", 1)
        image_ahead, ahead_grad = score_block(ahead_text, 0.0)
        image_behind, behind_grad = score_block(behind_text, 0.0)
        image_acc = image_acc + image_ahead + image_behind
        text_acc = text_acc + passed_along(ahead_grad.astype(jnp.bfloat16), "loop", offset).astype(
            ahead_grad.dtype
        )
        text_acc = text_acc + passed_along(
            behind_grad.astype(jnp.bfloat16), "loop", -offset
        ).astype(behind_grad.dtype)
    image_hat_grad = lax.psum_scatter(
        image_acc.astype(jnp.bfloat16), "pool", scatter_dimension=0, tiled=True
    ).astype(jnp.float32)
    image_grad = normalizer_reverse_pass(image_unit, image_inverse, image_hat_grad)
    text_grad = normalizer_reverse_pass(text_unit, text_inverse, text_acc)
    return (image_grad, text_grad)


def solution(mesh):
    return jax.shard_map(
        shards,
        mesh=mesh,
        in_specs=(P(("loop", "pool"), None), P(("loop", "pool"), None), P(), P()),
        out_specs=(P(("loop", "pool"), None), P(("loop", "pool"), None)),
        check_vma=False,
    )
```

profile of v0, /device:TPU:6, one launch (start us, length us, event | category | flops | bytes accessed | tf_op | source)
XLA Modules:
  0.0 158.9 jit_solution(6317111590661425119)
XLA Ops:
  8.3 1.8 %fusion.57 = bf16[128,1152]{1,0:T(8,128)(2,1)} fusion(bf16[128,1152]{1,0:T(8,128)(2,1)} %param.4, f32[128]{0:T(128)S(1)} %add_rsqrt_fusion.1), kind=kLoop, calls=%fused_computation.80 | loop fusion | flops 442368 | bytes 590336 | tf_op jit(solution)/shard_map/convert_element_type | solution.py:35
  12.4 1.9 %collective-permute-start.1 = (bf16[128,1152]{1,0:T(8,128)(2,1)S(1)}, bf16[128,1152]{1,0:T(8,128)(2,1)S(1)}, u32[]{:S(2)}, u32[]{:S(2)}) collective-permute-start(bf16[128,1152]{1,0:T(8,128)(2,1)S(1)} %fusion.55), channel_id=1, source_target_pairs={{0,8},{8,16},{16,24},{24,32},{32,40},{40,48},{48,56},{56,64},{64,7... | collective-permute-start | bytes 884744 | tf_op jit(solution)/shard_map/ppermute | solution.py:15
  14.3 11.7 %collective-permute-start = (bf16[128,1152]{1,0:T(8,128)(2,1)S(1)}, bf16[128,1152]{1,0:T(8,128)(2,1)S(1)}, u32[]{:S(2)}, u32[]{:S(2)}) collective-permute-start(bf16[128,1152]{1,0:T(8,128)(2,1)S(1)} %fusion.55), channel_id=1, source_target_pairs={{0,504},{8,0},{16,8},{24,16},{32,24},{40,32},{48,40},{56,48},{64,5... | collective-permute-start | bytes 884744 | tf_op jit(solution)/shard_map/ppermute | solution.py:15
  26.0 2.5 %collective-permute-done.1 = bf16[128,1152]{1,0:T(8,128)(2,1)S(1)} collective-permute-done((bf16[128,1152]{1,0:T(8,128)(2,1)S(1)}, bf16[128,1152]{1,0:T(8,128)(2,1)S(1)}, u32[]{:S(2)}, u32[]{:S(2)}) %collective-permute-start.1) | collective-permute-done | bytes 294944 | tf_op jit(solution)/shard_map/ppermute | solution.py:15
  28.5 1.9 %collective-permute-start.3 = (bf16[128,1152]{1,0:T(8,128)(2,1)S(1)}, bf16[128,1152]{1,0:T(8,128)(2,1)}, u32[]{:S(2)}, u32[]{:S(2)}) collective-permute-start(bf16[128,1152]{1,0:T(8,128)(2,1)S(1)} %collective-permute-done.1), channel_id=1, source_target_pairs={{0,8},{8,16},{16,24},{24,32},{32,40},{40,48},{48,56},{56,64},{64,7... | collective-permute-start | bytes 884744 | tf_op jit(solution)/shard_map/ppermute | solution.py:15
  30.4 7.3 %collective-permute-start.2 = (bf16[128,1152]{1,0:T(8,128)(2,1)S(1)}, bf16[128,1152]{1,0:T(8,128)(2,1)}, u32[]{:S(2)}, u32[]{:S(2)}) collective-permute-start(bf16[128,1152]{1,0:T(8,128)(2,1)S(1)} %collective-permute-done), channel_id=1, source_target_pairs={{0,504},{8,0},{16,8},{24,16},{32,24},{40,32},{48,40},{56,48},{64,5... | collective-permute-start | bytes 884744 | tf_op jit(solution)/shard_map/ppermute | solution.py:15
  40.3 1.9 %collective-permute-start.5 = (bf16[128,1152]{1,0:T(8,128)(2,1)}, bf16[128,1152]{1,0:T(8,128)(2,1)}, u32[]{:S(2)}, u32[]{:S(2)}) collective-permute-start(bf16[128,1152]{1,0:T(8,128)(2,1)} %collective-permute-done.3), channel_id=1, source_target_pairs={{0,8},{8,16},{16,24},{24,32},{32,40},{40,48},{48,56},{56,64},{64,7... | collective-permute-start | bytes 884744 | tf_op jit(solution)/shard_map/ppermute | solution.py:15
  42.3 7.3 %collective-permute-start.4 = (bf16[128,1152]{1,0:T(8,128)(2,1)}, bf16[128,1152]{1,0:T(8,128)(2,1)}, u32[]{:S(2)}, u32[]{:S(2)}) collective-permute-start(bf16[128,1152]{1,0:T(8,128)(2,1)} %collective-permute-done.2), channel_id=1, source_target_pairs={{0,504},{8,0},{16,8},{24,16},{32,24},{40,32},{48,40},{56,48},{64,5... | collective-permute-start | bytes 884744 | tf_op jit(solution)/shard_map/ppermute | solution.py:15
  49.5 19.0 %all-gather.2.cloned.1.call-done = bf16[1024,1152]{1,0:T(8,128)(2,1)} async-done(((bf16[128,1152]{1,0:T(8,128)(2,1)}), bf16[1024,1152]{1,0:T(8,128)(2,1)}) %all-gather.2.cloned.1.call-update) | async-done | bytes 2359312 | tf_op jit(solution)/shard_map/all_gather | solution.py:37
  68.5 2.5 %fusion.52 = bf16[1024,128]{1,0:T(8,128)(2,1)S(1)} fusion(bf16[1024,1152]{1,0:T(8,128)(2,1)} %all-gather.2.cloned.1.call-done, bf16[128,1152]{1,0:T(8,128)(2,1)S(1)} %fusion.55, s32[128]{0:T(128)S(1)} %iota_add_fusion, f32[]{:T(128)} %bitcast.51, f32[]{:T(128)} %bitcast.50), kind=kOutput, calls=%fused_computation.69 | convolution fusion | flops 303300608 | bytes 2916872 | tf_op jit(solution)/shard_map/id,jd->ij/dot_general | solution.py:43
  74.5 1.8 %fusion.66 = f32[1024,1152]{1,0:T(8,128)S(1)} fusion(bf16[1024,128]{1,0:T(8,128)(2,1)S(1)} %fusion.49, bf16[128,1152]{1,0:T(8,128)(2,1)} %collective-permute-done.3), kind=kOutput, calls=%fused_computation.94 | convolution fusion | flops 301989888 | bytes 5275648 | tf_op jit(solution)/shard_map/dot_general | solution.py:49
  79.6 1.8 %fusion.48 = bf16[1024,128]{1,0:T(8,128)(2,1)S(1)} fusion(bf16[1024,1152]{1,0:T(8,128)(2,1)S(1)} %copy-done, bf16[128,1152]{1,0:T(8,128)(2,1)} %collective-permute-done.2, f32[]{:T(128)} %bitcast.55, f32[]{:T(128)} %bitcast.44), kind=kOutput, calls=%fused_computation.65 | convolution fusion | flops 302907392 | bytes 2916360 | tf_op jit(solution)/shard_map/id,jd->ij/dot_general | solution.py:43
  84.9 1.8 %fusion.67 = f32[1024,1152]{1,0:T(8,128)S(1)} fusion(bf16[1024,128]{1,0:T(8,128)(2,1)S(1)} %fusion.51, bf16[128,1152]{1,0:T(8,128)(2,1)} %collective-permute-done.5), kind=kOutput, calls=%fused_computation.95 | convolution fusion | flops 301989888 | bytes 5275648 | tf_op jit(solution)/shard_map/dot_general | solution.py:49
  89.3 3.2 %fusion.2 = bf16[1024,1152]{1,0:T(8,128)(2,1)} fusion(f32[1024,1152]{1,0:T(8,128)S(1)} %fusion.67, f32[1024,1152]{1,0:T(8,128)S(1)} %fusion.1, bf16[1024,128]{1,0:T(8,128)(2,1)S(1)} %fusion.50, bf16[128,1152]{1,0:T(8,128)(2,1)} %collective-permute-done.4), kind=kOutput, calls=%fused_computation.6 | convolution fusion | flops 305528832 | bytes 12353536 | tf_op jit(solution)/shard_map/dot_general | solution.py:49
  94.1 2.1 %collective-permute-start.10 = (bf16[128,1152]{1,0:T(8,128)(2,1)S(1)}, bf16[128,1152]{1,0:T(8,128)(2,1)S(1)}, u32[]{:S(2)}, u32[]{:S(2)}) collective-permute-start(bf16[128,1152]{1,0:T(8,128)(2,1)S(1)} %convolution_convert_fusion.1), channel_id=1, source_target_pairs={{0,24},{8,32},{16,40},{24,48},{32,56},{40,64},{48,72},{56,80},{64,... | collective-permute-start | bytes 884744 | tf_op jit(solution)/shard_map/ppermute | solution.py:15
  96.7 8.2 %collective-permute-start.11 = (bf16[128,1152]{1,0:T(8,128)(2,1)S(1)}, bf16[128,1152]{1,0:T(8,128)(2,1)S(1)}, u32[]{:S(2)}, u32[]{:S(2)}) collective-permute-start(bf16[128,1152]{1,0:T(8,128)(2,1)S(1)} %convolution_convert_fusion), channel_id=1, source_target_pairs={{0,488},{8,496},{16,504},{24,0},{32,8},{40,16},{48,24},{56,32},{64... | collective-permute-start | bytes 884744 | tf_op jit(solution)/shard_map/ppermute | solution.py:15
  105.4 2.1 %collective-permute-start.8 = (bf16[128,1152]{1,0:T(8,128)(2,1)S(1)}, bf16[128,1152]{1,0:T(8,128)(2,1)S(1)}, u32[]{:S(2)}, u32[]{:S(2)}) collective-permute-start(bf16[128,1152]{1,0:T(8,128)(2,1)S(1)} %convolution_convert_fusion.3), channel_id=1, source_target_pairs={{0,16},{8,24},{16,32},{24,40},{32,48},{40,56},{48,64},{56,72},{64,... | collective-permute-start | bytes 884744 | tf_op jit(solution)/shard_map/ppermute | solution.py:15
  108.1 7.7 %collective-permute-start.9 = (bf16[128,1152]{1,0:T(8,128)(2,1)S(1)}, bf16[128,1152]{1,0:T(8,128)(2,1)S(1)}, u32[]{:S(2)}, u32[]{:S(2)}) collective-permute-start(bf16[128,1152]{1,0:T(8,128)(2,1)S(1)} %convolution_convert_fusion.2), channel_id=1, source_target_pairs={{0,496},{8,504},{16,0},{24,8},{32,16},{40,24},{48,32},{56,40},{64,... | collective-permute-start | bytes 884744 | tf_op jit(solution)/shard_map/ppermute | solution.py:15
  116.3 1.9 %collective-permute-start.6 = (bf16[128,1152]{1,0:T(8,128)(2,1)S(1)}, bf16[128,1152]{1,0:T(8,128)(2,1)S(1)}, u32[]{:S(2)}, u32[]{:S(2)}) collective-permute-start(bf16[128,1152]{1,0:T(8,128)(2,1)S(1)} %convolution_convert_fusion.5), channel_id=1, source_target_pairs={{0,8},{8,16},{16,24},{24,32},{32,40},{40,48},{48,56},{56,64},{64,7... | collective-permute-start | bytes 884744 | tf_op jit(solution)/shard_map/ppermute | solution.py:15
  118.8 7.4 %collective-permute-start.7 = (bf16[128,1152]{1,0:T(8,128)(2,1)S(1)}, bf16[128,1152]{1,0:T(8,128)(2,1)S(1)}, u32[]{:S(2)}, u32[]{:S(2)}) collective-permute-start(bf16[128,1152]{1,0:T(8,128)(2,1)S(1)} %convolution_convert_fusion.4), channel_id=1, source_target_pairs={{0,504},{8,0},{16,8},{24,16},{32,24},{40,32},{48,40},{56,48},{64,5... | collective-permute-start | bytes 884744 | tf_op jit(solution)/shard_map/ppermute | solution.py:15
  126.2 1.8 %collective-permute-done.6 = bf16[128,1152]{1,0:T(8,128)(2,1)S(1)} collective-permute-done((bf16[128,1152]{1,0:T(8,128)(2,1)S(1)}, bf16[128,1152]{1,0:T(8,128)(2,1)S(1)}, u32[]{:S(2)}, u32[]{:S(2)}) %collective-permute-start.6) | collective-permute-done | bytes 294944 | tf_op jit(solution)/shard_map/ppermute | solution.py:15
  128.1 2.4 %collective-permute-done.7 = bf16[128,1152]{1,0:T(8,128)(2,1)S(1)} collective-permute-done((bf16[128,1152]{1,0:T(8,128)(2,1)S(1)}, bf16[128,1152]{1,0:T(8,128)(2,1)S(1)}, u32[]{:S(2)}, u32[]{:S(2)}) %collective-permute-start.7) | collective-permute-done | bytes 294944 | tf_op jit(solution)/shard_map/ppermute | solution.py:15
  132.3 16.5 %reduce-scatter.2.cloned.1.call-done = bf16[128,1152]{1,0:T(8,128)(2,1)} async-done(((bf16[1024,1152]{1,0:T(8,128)(2,1)}), bf16[128,1152]{1,0:T(8,128)(2,1)}) %reduce-scatter.2.cloned.1.call-update) | async-done | bytes 294928 | tf_op jit(solution)/shard_map/reduce_scatter | solution.py:75
  150.1 2.0 %fusion.64 = f32[128,1152]{1,0:T(8,128)} fusion(bf16[128,1152]{1,0:T(8,128)(2,1)S(1)} %copy-done.2, bf16[128,1152]{1,0:T(8,128)(2,1)} %reduce-scatter.2.cloned.1.call-done, f32[128]{0:T(128)S(1)} %fusion.63, f32[128]{0:T(128)S(1)} %add_rsqrt_fusion.1), kind=kLoop, calls=%fused_computation.87 | loop fusion | flops 884736 | bytes 1180672 | tf_op jit(solution)/shard_map/mul | solution.py:26
  (57 shorter events, 24.8 us)
Async XLA Ops:
  7.2 61.3 %all-gather.2.cloned.1.call-start = ((), (), s32[]{:S(2)}) async-start(), calls=%async_computation.1 | async-start | bytes 2654208 | tf_op jit(solution)/shard_map/all_gather | solution.py:37
  10.1 138.7 %reduce-scatter.2.cloned.1.call-start = ((), (), s32[]{:S(2)}) async-start(), calls=%async_computation.2 | async-start | bytes 2654208 | tf_op jit(solution)/shard_map/reduce_scatter | solution.py:75
  12.4 16.1 %collective-permute-start.1 = (bf16[128,1152]{1,0:T(8,128)(2,1)S(1)}, bf16[128,1152]{1,0:T(8,128)(2,1)S(1)}, u32[]{:S(2)}, u32[]{:S(2)}) collective-permute-start(bf16[128,1152]{1,0:T(8,128)(2,1)S(1)} %fusion.55), channel_id=1, source_target_pairs={{0,8},{8,16},{16,24},{24,32},{32,40},{40,48},{48,56},{56,64},{64,7... | collective-permute-start | bytes 884744 | tf_op jit(solution)/shard_map/ppermute | solution.py:15
  14.3 16.1 %collective-permute-start = (bf16[128,1152]{1,0:T(8,128)(2,1)S(1)}, bf16[128,1152]{1,0:T(8,128)(2,1)S(1)}, u32[]{:S(2)}, u32[]{:S(2)}) collective-permute-start(bf16[128,1152]{1,0:T(8,128)(2,1)S(1)} %fusion.55), channel_id=1, source_target_pairs={{0,504},{8,0},{16,8},{24,16},{32,24},{40,32},{48,40},{56,48},{64,5... | collective-permute-start | bytes 884744 | tf_op jit(solution)/shard_map/ppermute | solution.py:15
  28.5 11.8 %collective-permute-start.3 = (bf16[128,1152]{1,0:T(8,128)(2,1)S(1)}, bf16[128,1152]{1,0:T(8,128)(2,1)}, u32[]{:S(2)}, u32[]{:S(2)}) collective-permute-start(bf16[128,1152]{1,0:T(8,128)(2,1)S(1)} %collective-permute-done.1), channel_id=1, source_target_pairs={{0,8},{8,16},{16,24},{24,32},{32,40},{40,48},{48,56},{56,64},{64,7... | collective-permute-start | bytes 884744 | tf_op jit(solution)/shard_map/ppermute | solution.py:15
  30.4 38.1 %copy-start.8 = (bf16[128,1152]{1,0:T(8,128)(2,1)}, bf16[128,1152]{1,0:T(8,128)(2,1)S(1)}, u32[]{:S(2)}) copy-start(bf16[128,1152]{1,0:T(8,128)(2,1)S(1)} %collective-permute-done) | copy-start | bytes 884740
  30.4 11.8 %collective-permute-start.2 = (bf16[128,1152]{1,0:T(8,128)(2,1)S(1)}, bf16[128,1152]{1,0:T(8,128)(2,1)}, u32[]{:S(2)}, u32[]{:S(2)}) collective-permute-start(bf16[128,1152]{1,0:T(8,128)(2,1)S(1)} %collective-permute-done), channel_id=1, source_target_pairs={{0,504},{8,0},{16,8},{24,16},{32,24},{40,32},{48,40},{56,48},{64,5... | collective-permute-start | bytes 884744 | tf_op jit(solution)/shard_map/ppermute | solution.py:15
  40.3 42.8 %collective-permute-start.5 = (bf16[128,1152]{1,0:T(8,128)(2,1)}, bf16[128,1152]{1,0:T(8,128)(2,1)}, u32[]{:S(2)}, u32[]{:S(2)}) collective-permute-start(bf16[128,1152]{1,0:T(8,128)(2,1)} %collective-permute-done.3), channel_id=1, source_target_pairs={{0,8},{8,16},{16,24},{24,32},{32,40},{40,48},{48,56},{56,64},{64,7... | collective-permute-start | bytes 884744 | tf_op jit(solution)/shard_map/ppermute | solution.py:15
  42.3 44.5 %collective-permute-start.4 = (bf16[128,1152]{1,0:T(8,128)(2,1)}, bf16[128,1152]{1,0:T(8,128)(2,1)}, u32[]{:S(2)}, u32[]{:S(2)}) collective-permute-start(bf16[128,1152]{1,0:T(8,128)(2,1)} %collective-permute-done.2), channel_id=1, source_target_pairs={{0,504},{8,0},{16,8},{24,16},{32,24},{40,32},{48,40},{56,48},{64,5... | collective-permute-start | bytes 884744 | tf_op jit(solution)/shard_map/ppermute | solution.py:15
  71.0 1.7 %copy-start = (bf16[1024,1152]{1,0:T(8,128)(2,1)S(1)}, bf16[1024,1152]{1,0:T(8,128)(2,1)}, u32[]{:S(2)}) copy-start(bf16[1024,1152]{1,0:T(8,128)(2,1)} %all-gather.2.cloned.1.call-done) | copy-start | bytes 7077892
  74.5 1.9 %copy-start.3 = (bf16[1024,128]{1,0:T(8,128)(2,1)}, bf16[1024,128]{1,0:T(8,128)(2,1)S(1)}, u32[]{:S(2)}) copy-start(bf16[1024,128]{1,0:T(8,128)(2,1)S(1)} %fusion.49) | copy-start | bytes 786436
  74.5 1.9 %copy-start.9 = (bf16[128,1152]{1,0:T(8,128)(2,1)S(1)}, bf16[128,1152]{1,0:T(8,128)(2,1)}, u32[]{:S(2)}) copy-start(bf16[128,1152]{1,0:T(8,128)(2,1)} %copy-done.8) | copy-start | bytes 884740
  84.9 1.8 %copy-start.5 = (bf16[1024,128]{1,0:T(8,128)(2,1)}, bf16[1024,128]{1,0:T(8,128)(2,1)S(1)}, u32[]{:S(2)}) copy-start(bf16[1024,128]{1,0:T(8,128)(2,1)S(1)} %fusion.51) | copy-start | bytes 786436
  88.5 0.7 copy-start.7
  92.5 3.6 %copy-start.6 = (bf16[1024,128]{1,0:T(8,128)(2,1)S(1)}, bf16[1024,128]{1,0:T(8,128)(2,1)}, u32[]{:S(2)}) copy-start(bf16[1024,128]{1,0:T(8,128)(2,1)} %copy-done.5) | copy-start | bytes 786436
  94.1 13.5 %copy-start.4 = (bf16[1024,128]{1,0:T(8,128)(2,1)S(1)}, bf16[1024,128]{1,0:T(8,128)(2,1)}, u32[]{:S(2)}) copy-start(bf16[1024,128]{1,0:T(8,128)(2,1)} %copy-done.3) | copy-start | bytes 786436
  94.1 24.7 %collective-permute-start.10 = (bf16[128,1152]{1,0:T(8,128)(2,1)S(1)}, bf16[128,1152]{1,0:T(8,128)(2,1)S(1)}, u32[]{:S(2)}, u32[]{:S(2)}) collective-permute-start(bf16[128,1152]{1,0:T(8,128)(2,1)S(1)} %convolution_convert_fusion.1), channel_id=1, source_target_pairs={{0,24},{8,32},{16,40},{24,48},{32,56},{40,64},{48,72},{56,80},{64,... | collective-permute-start | bytes 884744 | tf_op jit(solution)/shard_map/ppermute | solution.py:15
  96.7 29.5 %collective-permute-start.11 = (bf16[128,1152]{1,0:T(8,128)(2,1)S(1)}, bf16[128,1152]{1,0:T(8,128)(2,1)S(1)}, u32[]{:S(2)}, u32[]{:S(2)}) collective-permute-start(bf16[128,1152]{1,0:T(8,128)(2,1)S(1)} %convolution_convert_fusion), channel_id=1, source_target_pairs={{0,488},{8,496},{16,504},{24,0},{32,8},{40,16},{48,24},{56,32},{64... | collective-permute-start | bytes 884744 | tf_op jit(solution)/shard_map/ppermute | solution.py:15
  105.4 20.8 %collective-permute-start.8 = (bf16[128,1152]{1,0:T(8,128)(2,1)S(1)}, bf16[128,1152]{1,0:T(8,128)(2,1)S(1)}, u32[]{:S(2)}, u32[]{:S(2)}) collective-permute-start(bf16[128,1152]{1,0:T(8,128)(2,1)S(1)} %convolution_convert_fusion.3), channel_id=1, source_target_pairs={{0,16},{8,24},{16,32},{24,40},{32,48},{40,56},{48,64},{56,72},{64,... | collective-permute-start | bytes 884744 | tf_op jit(solution)/shard_map/ppermute | solution.py:15
  108.1 22.4 %copy-start.1 = (bf16[128,1152]{1,0:T(8,128)(2,1)S(1)}, bf16[128,1152]{1,0:T(8,128)(2,1)}, u32[]{:S(2)}) copy-start(bf16[128,1152]{1,0:T(8,128)(2,1)} %param.5) | copy-start | bytes 884740
  108.1 18.2 %collective-permute-start.9 = (bf16[128,1152]{1,0:T(8,128)(2,1)S(1)}, bf16[128,1152]{1,0:T(8,128)(2,1)S(1)}, u32[]{:S(2)}, u32[]{:S(2)}) collective-permute-start(bf16[128,1152]{1,0:T(8,128)(2,1)S(1)} %convolution_convert_fusion.2), channel_id=1, source_target_pairs={{0,496},{8,504},{16,0},{24,8},{32,16},{40,24},{48,32},{56,40},{64,... | collective-permute-start | bytes 884744 | tf_op jit(solution)/shard_map/ppermute | solution.py:15
  116.3 11.8 %collective-permute-start.6 = (bf16[128,1152]{1,0:T(8,128)(2,1)S(1)}, bf16[128,1152]{1,0:T(8,128)(2,1)S(1)}, u32[]{:S(2)}, u32[]{:S(2)}) collective-permute-start(bf16[128,1152]{1,0:T(8,128)(2,1)S(1)} %convolution_convert_fusion.5), channel_id=1, source_target_pairs={{0,8},{8,16},{16,24},{24,32},{32,40},{40,48},{48,56},{56,64},{64,7... | collective-permute-start | bytes 884744 | tf_op jit(solution)/shard_map/ppermute | solution.py:15
  118.8 30.1 %copy-start.2 = (bf16[128,1152]{1,0:T(8,128)(2,1)S(1)}, bf16[128,1152]{1,0:T(8,128)(2,1)}, u32[]{:S(2)}) copy-start(bf16[128,1152]{1,0:T(8,128)(2,1)} %param.4) | copy-start | bytes 884740
  118.8 11.7 %collective-permute-start.7 = (bf16[128,1152]{1,0:T(8,128)(2,1)S(1)}, bf16[128,1152]{1,0:T(8,128)(2,1)S(1)}, u32[]{:S(2)}, u32[]{:S(2)}) collective-permute-start(bf16[128,1152]{1,0:T(8,128)(2,1)S(1)} %convolution_convert_fusion.4), channel_id=1, source_target_pairs={{0,504},{8,0},{16,8},{24,16},{32,24},{40,32},{48,40},{56,48},{64,5... | collective-permute-start | bytes 884744 | tf_op jit(solution)/shard_map/ppermute | solution.py:15
Sparse Core Ops, SparseCore 0:
  10.7 57.8 all-gather.1
  92.6 56.1 reduce-scatter.1
where the time goes:
time: 160 us; the launch traced here: 159 us
  starting transfers between devices  61.3 us (38%)
  waiting for transfers between devices  43.6 us (27%)
  matrix products  27.3 us (17%)
  between operations  15.7 us (10%)
  other arithmetic  9.35 us (6%)
  local copies, waits for them, and re-layouts  1.64 us (1%)
    ppermute x12, starting transfers between devices, passed_along(): return lax.ppermute(value, axis, pairs)  61.2 us
    all_gather x1, waiting for transfers between devices, shards(): pooled = lax.all_gather(picture_direction, 'pool', axis=0, tiled=True)  19 us
    reduce_scatter x1, waiting for transfers between devices, shards(): lax.psum_scatter(image_acc.astype(jnp.bfloat16), 'pool', scatter_dimensio...  16.5 us
    dot_general x7, matrix products, score_block(): jnp.einsum('id,jd->ij', pooled, text_tile_rows, preferred_element_type=jn...  11.3 us
    dot_general x7, matrix products, score_block(): jnp.dot(weight_brain_float, text_tile_rows, preferred_element_type=jnp.fl...  10.9 us
    ppermute x12, waiting for transfers between devices, passed_along(): return lax.ppermute(value, axis, pairs)  8.05 us
    dot_general x7, matrix products, score_block(): jnp.einsum('ij,id->jd', weight_brain_float, pooled, preferred_element_typ...  5.08 us
  transfers between devices with their start and end apart: 14, of which 6 were waited for; matrix products, arithmetic and copies ran while one was open for 16% of the time, Pallas kernels for 0%

commit v1 on v0

v1 whole, which is shorter than its diff:
```python
import jax
import jax.numpy as jnp
from jax import lax
from jax.experimental import pallas as pl
from jax.experimental.pallas import tpu as pltpu
from jax.sharding import PartitionSpec as P

MESH = pl.DeviceIdType.MESH
epsilon_norm = 1e-06

STEPS = 4
REACH = STEPS - 1
TEXTS = 2 * REACH + 1

COPIES = (
    "x", "own+", "own-", "part+", "part-", "fwd+", "fwd-", "pfwd+", "pfwd-",
    "tsib", "tz+", "tz-", "tfar", "tsib+", "tsib-",
    "half+", "half-", "phalf+", "phalf-", "pfull+", "pfull-", "full+", "full-", "xsum",
    "gsib", "gsib+", "gsib-", "gz+", "gz-", "gfar",
)
NUMBER = {name: i for i, name in enumerate(COPIES)}


def inverse_norm(wide):
    return lax.rsqrt(jnp.sum(wide * wide, axis=-1, keepdims=True) + epsilon_norm)


def kernel(
    sharp_ref, shift_ref, pic_ref, cap_ref, pic_out, cap_out,
    img, txt, weights, part, tgrad, isend, ihalf, ifull, tsend, trecv, send_sem, recv_sem,
):
    rows, width = pic_ref.shape
    half = rows // 2
    n_loop = lax.axis_size("loop")
    group, cls = lax.axis_index("loop"), lax.axis_index("pool")
    sign = 1 - 2 * lax.rem(group, 2)
    n_y = lax.axis_size("pool") // 2
    x, y = cls // n_y, lax.rem(cls, n_y)
    x_dev = (group, (1 - x) * n_y + y)
    up = (group, x * n_y + lax.rem(y + 1, n_y))
    down = (group, x * n_y + lax.rem(y + n_y - 1, n_y))
    ahead = (lax.rem(group + 2, n_loop), cls)
    behind = (lax.rem(group + n_loop - 2, n_loop), cls)
    sibling = (group + sign, cls)
    far = (lax.rem(group + n_loop - 3 * sign, n_loop), cls)
    peers = (x_dev, up, down, ahead, behind, sibling, far)

    barrier = pltpu.get_barrier_semaphore()
    for peer in peers:
        pl.semaphore_signal(barrier, inc=1, device_id=peer, device_id_type=MESH)

    def block(ref, slot, start=0, size=rows):
        first = slot * rows + start
        if not isinstance(first, int):
            first = pl.multiple_of(first, 16)
        return ref.at[pl.ds(first, size)]

    copies = {}

    def send(name, src, dst, device):
        n = NUMBER[name]
        copies[name] = pltpu.make_async_remote_copy(
            src_ref=src, dst_ref=dst, send_sem=send_sem.at[n], recv_sem=recv_sem.at[n],
            device_id=device, device_id_type=MESH,
        )
        copies[name].start()

    def arrived(*names):
        for name in names:
            copies[name].wait_recv()

    sharp, shift = sharp_ref[0], shift_ref[0]

    def unit_of(ref):
        wide = ref[...].astype(jnp.float32)
        inverse = inverse_norm(wide)
        return wide * inverse, inverse

    img[0:rows] = unit_of(pic_ref)[0].astype(jnp.bfloat16)
    own_text = REACH * rows
    txt[own_text : own_text + rows] = unit_of(cap_ref)[0].astype(jnp.bfloat16)

    pl.semaphore_wait(barrier, len(peers))

    send("x", block(img, 0), block(img, 1), x_dev)
    send("own+", block(img, 0), block(img, 3), up)
    send("own-", block(img, 0), block(img, 2), down)
    send("tsib", block(txt, REACH), block(txt, REACH - sign), sibling)
    send("tz+", block(txt, REACH), block(txt, REACH - 2), ahead)
    send("tz-", block(txt, REACH), block(txt, REACH + 2), behind)
    send("tfar", block(txt, REACH), block(txt, REACH + 3 * sign), far)

    arrived("x")
    send("part+", block(img, 1), block(img, 5), up)
    send("part-", block(img, 1), block(img, 4), down)
    arrived("own+", "own-")
    send("fwd+", block(img, 3, 0, half), block(img, 6, 0, half), up)
    send("fwd-", block(img, 2, half, half), block(img, 6, half, half), down)
    arrived("tz+", "tz-")
    send("tsib-", block(txt, REACH - 2), block(txt, REACH - 2 - sign), sibling)
    send("tsib+", block(txt, REACH + 2), block(txt, REACH + 2 - sign), sibling)
    arrived("tsib", "tsib-", "tsib+", "tfar")

    def score(pair):
        first = 2 * pair * rows
        here = pl.ds(first, 2 * rows)
        dots = lax.dot_general(
            img[here], txt[...], (((1,), (1,)), ((), ())), preferred_element_type=jnp.float32
        )
        chance = 1.0 / (1.0 + jnp.exp(-(sharp * dots + shift)))
        if pair == 0:
            i = lax.broadcasted_iota(jnp.int32, chance.shape, 0)
            j = lax.broadcasted_iota(jnp.int32, chance.shape, 1)
            chance = chance - ((i + own_text == j) & (i < rows)).astype(jnp.float32)
        weight = (sharp * chance).astype(jnp.bfloat16)
        weights[here] = weight
        part[here] = jnp.dot(weight, txt[...], preferred_element_type=jnp.float32)

    def text_grad(first, size):
        here = pl.ds(first * rows, size * rows)
        return lax.dot_general(
            weights[here], img[here], (((0,), (0,)), ((), ())), preferred_element_type=jnp.float32
        )

    score(0)
    score(1)
    arrived("part+", "part-")
    send("pfwd+", block(img, 5, 0, half), block(img, 7, 0, half), up)
    send("pfwd-", block(img, 4, half, half), block(img, 7, half, half), down)
    score(2)
    tgrad[...] = text_grad(0, 6)
    arrived("fwd+", "fwd-", "pfwd+", "pfwd-")
    score(3)

    def take(slot, start=0, size=rows):
        return part[slot * rows + start : slot * rows + start + size]

    def put(slot, value, start=0):
        first = slot * rows + start
        isend[first : first + value.shape[0]] = value.astype(jnp.bfloat16)

    put(6, take(6))
    put(7, take(7))
    send("phalf+", block(isend, 7, 0, half), block(ihalf, 0, 0, half), up)
    send("phalf-", block(isend, 7, half, half), block(ihalf, 0, half, half), down)
    send("half+", block(isend, 6, 0, half), block(ihalf, 1, 0, half), up)
    send("half-", block(isend, 6, half, half), block(ihalf, 1, half, half), down)

    tgrad[...] += text_grad(6, 2)

    def grad_rows(slot):
        return tgrad[pl.ds(pl.multiple_of(slot * rows, rows), rows)]

    def put_text(n, value):
        tsend[n * rows : (n + 1) * rows] = value.astype(jnp.bfloat16)

    def got_text(n):
        return trecv[n * rows : (n + 1) * rows].astype(jnp.float32)

    put_text(1, grad_rows(REACH + sign - 2))
    send("gsib-", block(tsend, 1), block(trecv, 1), sibling)
    put_text(2, grad_rows(REACH + sign + 2))
    send("gsib+", block(tsend, 2), block(trecv, 2), sibling)
    put_text(5, grad_rows(REACH - 3 * sign))
    send("gfar", block(tsend, 5), block(trecv, 5), far)
    put_text(0, grad_rows(REACH + sign))
    send("gsib", block(tsend, 0), block(trecv, 0), sibling)

    def got_half(n, start):
        first = n * rows + start
        return ihalf[first : first + half].astype(jnp.float32)

    arrived("phalf+", "phalf-")
    put(4, take(4, 0, half) + got_half(0, 0))
    put(4, take(4, half, half), half)
    send("pfull+", block(isend, 4), block(ifull, 0), up)
    put(5, take(5, 0, half))
    put(5, take(5, half, half) + got_half(0, half), half)
    send("pfull-", block(isend, 5), block(ifull, 1), down)

    arrived("gsib-")
    put_text(3, grad_rows(REACH - 2) + got_text(1))
    send("gz-", block(tsend, 3), block(trecv, 4), behind)
    arrived("gsib+")
    put_text(4, grad_rows(REACH + 2) + got_text(2))
    send("gz+", block(tsend, 4), block(trecv, 3), ahead)

    arrived("half+", "half-")
    put(2, take(2, 0, half) + got_half(1, 0))
    put(2, take(2, half, half), half)
    send("full+", block(isend, 2), block(ifull, 2), up)
    put(3, take(3, 0, half))
    put(3, take(3, half, half) + got_half(1, half), half)
    send("full-", block(isend, 3), block(ifull, 3), down)

    def got_full(n):
        return ifull[n * rows : (n + 1) * rows].astype(jnp.float32)

    def back(ref, grad_hat):
        unit, inverse = unit_of(ref)
        inner = jnp.sum(unit * grad_hat, axis=-1, keepdims=True)
        return inverse * (grad_hat - unit * inner)

    arrived("pfull+", "pfull-")
    put(1, take(1) + got_full(0) + got_full(1))
    send("xsum", block(isend, 1), block(ifull, 4), x_dev)

    arrived("gsib", "gz-", "gz+", "gfar")
    text_hat_grad = grad_rows(REACH) + got_text(0) + got_text(3) + got_text(4) + got_text(5)
    cap_out[...] = back(cap_ref, text_hat_grad)

    arrived("full+", "full-", "xsum")
    image_hat_grad = take(0) + got_full(2) + got_full(3) + got_full(4)
    pic_out[...] = back(pic_ref, image_hat_grad)

    for name in COPIES:
        copies[name].wait_send()


def shards(picture_embedding_raw, caption_embedding_raw, score_sharpness, score_shift_term):
    rows, width = picture_embedding_raw.shape
    n_pool = lax.axis_size("pool")
    result = jax.ShapeDtypeStruct((rows, width), jnp.float32)

    def blocks(count, dtype=jnp.bfloat16):
        return pltpu.VMEM((count * rows, width), dtype)

    vmem = pl.BlockSpec(memory_space=pltpu.VMEM)
    smem = pl.BlockSpec(memory_space=pltpu.SMEM)
    return pl.pallas_call(
        kernel,
        out_shape=(result, result),
        in_specs=[smem, smem, vmem, vmem],
        out_specs=(vmem, vmem),
        scratch_shapes=[
            blocks(n_pool),
            blocks(TEXTS),
            pltpu.VMEM((n_pool * rows, TEXTS * rows), jnp.bfloat16),
            blocks(n_pool, jnp.float32),
            blocks(TEXTS, jnp.float32),
            blocks(n_pool),
            blocks(2),
            blocks(5),
            blocks(6),
            blocks(6),
            pltpu.SemaphoreType.DMA((len(COPIES),)),
            pltpu.SemaphoreType.DMA((len(COPIES),)),
        ],
        compiler_params=pltpu.CompilerParams(
            collective_id=0, has_side_effects=True, vmem_limit_bytes=56 * 2**20
        ),
    )(score_sharpness, score_shift_term, picture_embedding_raw, caption_embedding_raw)


def solution(mesh):
    return jax.shard_map(
        shards,
        mesh=mesh,
        in_specs=(P(("loop", "pool"), None), P(("loop", "pool"), None), P(), P()),
        out_specs=(P(("loop", "pool"), None), P(("loop", "pool"), None)),
        check_vma=False,
    )
```

time: 160 us -> 75.8 us (0.47)
  Pallas kernels: 0 us -> 70.9 us
  starting transfers between devices: 61.3 us -> 0 us
  waiting for transfers between devices: 43.6 us -> 0 us
  matrix products: 27.3 us -> 0 us
  between operations: 15.7 us -> 1.94 us
  other arithmetic: 9.35 us -> 0 us
    pallas_call x0 -> x1, Pallas kernels: none -> 70.9 us  [shards(): pl.pallas_call(kernel, out_shape=(result, result), in_specs=[smem, smem,...]
    ppermute x12 -> x0, starting transfers between devices: 61.2 us -> none  [passed_along(): return lax.ppermute(value, axis, pairs)]
    dot_general x21 -> x0, matrix products: 27.3 us -> none  [the longest x7 11.3 us: score_block(): jnp.einsum('id,jd->ij', pooled, text_tile_rows, preferred_element_type=jn...]
    all_gather x1 -> x0, waiting for transfers between devices: 19 us -> none  [shards(): pooled = lax.all_gather(picture_direction, 'pool', axis=0, tiled=True)]
    reduce_scatter x1 -> x0, waiting for transfers between devices: 16.5 us -> none  [shards(): lax.psum_scatter(image_acc.astype(jnp.bfloat16), 'pool', scatter_dimensio...]
    ppermute x12 -> x0, waiting for transfers between devices: 8.05 us -> none  [passed_along(): return lax.ppermute(value, axis, pairs)]
    reduce_sum x3 -> x0, other arithmetic: 3.41 us -> none  [the longest x2 2.21 us: normalize(): jnp.sum(wide * wide, axis=-1, keepdims=True) + epsilon_norm]
    mul x2 -> x0, other arithmetic: 3.03 us -> none  [normalizer_reverse_pass(): return inverse * (grad_hat - unit_rows * inner)]
  transfers between devices with their start and end apart: 14 -> 0, of which waited for: 6 -> 0; matrix products, arithmetic and copies ran while one was open for 16% -> 0% of each run, Pallas kernels for 0% -> 0%
where the time goes in v1:
time: 75.8 us; the launch traced here: 75.6 us
  Pallas kernels  70.9 us (94%)
  local copies, waits for them, and re-layouts  2.8 us (4%)
  between operations  1.94 us (3%)
    pallas_call x1, Pallas kernels, shards(): pl.pallas_call(kernel, out_shape=(result, result), in_specs=[smem, smem,...  70.9 us
    unnamed x4, local copies, waits for them, and re-layouts  2.8 us

profile of v1, /device:TPU:6, one launch (start us, length us, event | category | flops | bytes accessed | tf_op | source)
XLA Modules:
  0.0 75.6 jit_solution(14790429371409246488)
XLA Ops:
  1.9 70.9 %shard_map.59 = (f32[128,1152]{1,0:T(8,128)}, f32[128,1152]{1,0:T(8,128)}) custom-call(f32[1]{0:T(128)S(6)} %copy.8.sharp_ref, f32[1]{0:T(128)S(6)} %copy.9.shift_ref, bf16[128,1152]{1,0:T(8,128)(2,1)} %pic_ref.1, bf16[128,1152]{1,0:T(8,128)(2,1)} %cap_ref.1), custom_call_target="tpu_custom_call" | custom-call | tf_op jit(solution)/shard_map/pallas_call | solution.py:230
  72.8 0.0 copy-start
  72.8 2.0 %copy.10 = f32[128,1152]{1,0:T(8,128)} copy(f32[128,1152]{1,0:T(8,128)} %get-tuple-element.4) | data formatting | bytes 1179648
  74.8 0.0 copy-done
  74.8 0.8 %copy.11 = f32[128,1152]{1,0:T(8,128)} copy(f32[128,1152]{1,0:T(8,128)S(1)} %copy-done) | data formatting | bytes 1179648
Async XLA Ops:
  72.8 2.0 %copy-start = (f32[128,1152]{1,0:T(8,128)S(1)}, f32[128,1152]{1,0:T(8,128)}, u32[]{:S(2)}) copy-start(f32[128,1152]{1,0:T(8,128)} %get-tuple-element.5) | copy-start | bytes 1769476

commit v2 on v1

v2 whole, which is shorter than its diff:
```python
import jax
import jax.numpy as jnp
from jax import lax
from jax.experimental import pallas as pl
from jax.experimental.pallas import tpu as pltpu
from jax.sharding import PartitionSpec as P

MESH = pl.DeviceIdType.MESH
epsilon_norm = 1e-06

TEXTS = 7
EARLY = 4

COPIES = (
    "x0", "x1", "own+0", "own+1", "own-0", "own-1", "part+0", "part+1", "part-0", "part-1",
    "fwd+", "fwd-", "pfwd+", "pfwd-",
    "tsib", "tfirst", "tsecond", "tfar", "tsib1", "tsib2",
    "half+", "half-", "phalf+", "phalf-", "pfull+0", "pfull+1", "pfull-0", "pfull-1",
    "full+0", "full+1", "full-0", "full-1", "xsum",
    "gsib", "gsib1", "gsib2", "gfirst", "gsecond", "gfar",
)
NUMBER = {name: i for i, name in enumerate(COPIES)}


def inverse_norm(wide):
    return lax.rsqrt(jnp.sum(wide * wide, axis=-1, keepdims=True) + epsilon_norm)


def unit_of(ref):
    wide = ref[...].astype(jnp.float32)
    inverse = inverse_norm(wide)
    return wide * inverse, inverse


def kernel(
    sharp_ref, shift_ref, pic_ref, cap_ref, pic_out, cap_out,
    pic, cap, img, txt, weights, part, tgrad, isend, ihalf, ifull, tsend, trecv,
    send_sem, recv_sem, load_sem,
):
    rows, width = pic_ref.shape
    loads = [
        pltpu.make_async_copy(ref, dst, load_sem.at[n])
        for n, (ref, dst) in enumerate(((pic_ref, pic), (cap_ref, cap)))
    ]
    for load in loads:
        load.start()
    half = rows // 2
    n_loop = lax.axis_size("loop")
    n_z = n_loop // 4
    group, cls = lax.axis_index("loop"), lax.axis_index("pool")
    sign = 1 - 2 * lax.rem(group, 2)
    z = lax.rem(group // 2, n_z)
    n_y = lax.axis_size("pool") // 2
    x, y = cls // n_y, lax.rem(cls, n_y)
    x_dev = (group, (1 - x) * n_y + y)
    up = (group, x * n_y + lax.rem(y + 1, n_y))
    down = (group, x * n_y + lax.rem(y + n_y - 1, n_y))
    toward = jnp.where(z == n_z - 1, -2, 2)
    first = (lax.rem(group + n_loop + toward, n_loop), cls)
    at_first = jnp.where(z >= n_z - 2, 0, 1)
    across = (z == 0) | (z == n_z - 1)
    at_second = jnp.where(across, 1, 0)
    sibling = (group + sign, cls)
    far_across = jnp.where(sign > 0, z == 0, z == n_z - 1)
    by_first = sign * 2 == toward
    mirror = (1 - x) * n_y + y
    second = (lax.rem(group + n_loop - toward, n_loop), jnp.where(across, mirror, cls))
    far = (lax.rem(group + n_loop - sign, n_loop), jnp.where(far_across, mirror, cls))
    low = z == 0
    beyond = across.astype(jnp.int32) + far_across.astype(jnp.int32)

    barrier = pltpu.get_barrier_semaphore()

    def greet(peer):
        pl.semaphore_signal(barrier, inc=1, device_id=peer, device_id_type=MESH)

    def greet_across():
        @pl.when(across)
        def _():
            greet(second)

        @pl.when(far_across)
        def _():
            greet(far)

    for peer in (x_dev, up, down, first, sibling):
        greet(peer)

    @pl.when(jnp.logical_not(across))
    def _():
        greet(second)

    @pl.when(jnp.logical_not(far_across))
    def _():
        greet(far)

    def block(ref, slot, start=0, size=rows):
        begin = slot * rows + start
        if not isinstance(begin, int):
            begin = pl.multiple_of(begin, rows)
        return ref.at[pl.ds(begin, size)]

    copies = {}

    def make(name, src, dst, device, lands=0):
        n = NUMBER[name]
        copies[name] = pltpu.make_async_remote_copy(
            src_ref=src, dst_ref=dst, send_sem=send_sem.at[n], recv_sem=recv_sem.at[n + lands],
            device_id=device, device_id_type=MESH,
        )
        return copies[name]

    def send(name, src, dst, device, lands=0):
        make(name, src, dst, device, lands).start()

    def arrived(*names):
        for name in names:
            copies[name].wait_recv()

    def came(name, dst):
        n = NUMBER[name]
        pltpu.make_async_remote_copy(
            src_ref=dst, dst_ref=dst, send_sem=send_sem.at[n], recv_sem=recv_sem.at[n],
            device_id=first, device_id_type=MESH,
        ).wait_recv()

    loads[0].wait()
    img[0:rows] = unit_of(pic)[0].astype(jnp.bfloat16)
    loads[1].wait()
    txt[0:rows] = unit_of(cap)[0].astype(jnp.bfloat16)
    sharp, shift = sharp_ref[0], shift_ref[0]

    pl.semaphore_wait(barrier, jnp.where(low, 7 - beyond, 7))
    greet_across()

    def half_of(ref, slot, n):
        return block(ref, slot, n * half, half)

    def move(name, n, ref, slot, dst, dst_slot, device):
        send(name, half_of(ref, slot, n), half_of(dst, dst_slot, n), device)

    move("x0", 0, img, 0, img, 1, x_dev)
    move("own+0", 0, img, 0, img, 3, up)
    move("own-1", 1, img, 0, img, 2, down)
    send("tsib", block(txt, 0), block(txt, 1), sibling)
    make("tsecond", block(txt, 0), block(txt, 2 + 2 * at_second), second, at_second - 1)
    make("tfar", block(txt, jnp.where(by_first, 2, 4)), block(txt, 6), far)

    @pl.when(jnp.logical_not(low & across))
    def _():
        copies["tsecond"].start()

    send("tfirst", block(txt, 0), block(txt, 2 + 2 * at_first), first, at_first)
    move("own+1", 1, img, 0, img, 3, up)
    move("own-0", 0, img, 0, img, 2, down)

    arrived("x0")
    move("x1", 1, img, 0, img, 1, x_dev)
    move("part+0", 0, img, 1, img, 5, up)
    move("part-0", 0, img, 1, img, 4, down)
    arrived("own+0", "own-1")
    move("fwd+", 0, img, 3, img, 6, up)
    move("fwd-", 1, img, 2, img, 6, down)

    arrived("x1")
    move("part-1", 1, img, 1, img, 4, down)
    move("part+1", 1, img, 1, img, 5, up)
    came("tfirst", block(txt, 2))
    send("tsib1", block(txt, 2), block(txt, 3), sibling)

    @pl.when(by_first & jnp.logical_not(low & far_across))
    def _():
        copies["tfar"].start()

    make("tsib2", block(txt, 4), block(txt, 5), sibling)

    def second_text():
        came("tsecond", block(txt, 4))
        copies["tsib2"].start()

        @pl.when(jnp.logical_not(by_first))
        def _():
            copies["tfar"].start()

    @pl.when(jnp.logical_not(across))
    def _():
        second_text()

    arrived("own+1", "own-0", "tsib", "tsib1")

    def score(slot, count, begin, end):
        here = pl.ds(slot * rows, count * rows)
        dots = lax.dot_general(
            img[here], txt[begin * rows : end * rows], (((1,), (1,)), ((), ())),
            preferred_element_type=jnp.float32,
        )
        chance = 1.0 / (1.0 + jnp.exp(-(sharp * dots + shift)))
        if slot == 0 and begin == 0:
            i = lax.broadcasted_iota(jnp.int32, chance.shape, 0)
            j = lax.broadcasted_iota(jnp.int32, chance.shape, 1)
            chance = chance - ((i == j) & (i < rows)).astype(jnp.float32)
        weights[here, begin * rows : end * rows] = (sharp * chance).astype(jnp.bfloat16)

    def image_grad(slot, count):
        here = pl.ds(slot * rows, count * rows)
        part[here] = jnp.dot(weights[here], txt[...], preferred_element_type=jnp.float32)

    def text_grad(begin, end):
        tgrad[begin * rows : end * rows] = lax.dot_general(
            weights[:, begin * rows : end * rows], img[...], (((0,), (0,)), ((), ())),
            preferred_element_type=jnp.float32,
        )

    def take(slot, start=0, size=rows):
        return part[slot * rows + start : slot * rows + start + size]

    def put(slot, value, start=0):
        begin = slot * rows + start
        isend[begin : begin + value.shape[0]] = value.astype(jnp.bfloat16)

    score(0, 4, 0, EARLY)
    arrived("part+0", "part-1")
    move("pfwd+", 0, img, 5, img, 7, up)
    move("pfwd-", 1, img, 4, img, 7, down)
    arrived("part+1", "part-0")
    score(4, 2, 0, EARLY)

    @pl.when(low & (beyond > 0))
    def _():
        pl.semaphore_wait(barrier, beyond)

        @pl.when(across)
        def _():
            copies["tsecond"].start()

        @pl.when(far_across)
        def _():
            copies["tfar"].start()

    @pl.when(across)
    def _():
        second_text()

    arrived("fwd+", "fwd-", "pfwd+", "pfwd-")
    score(6, 2, 0, EARLY)

    arrived("tsib2", "tfar")
    score(6, 2, EARLY, TEXTS)
    image_grad(6, 2)
    put(7, take(7))
    move("phalf+", 0, isend, 7, ihalf, 0, up)
    move("phalf-", 1, isend, 7, ihalf, 0, down)
    put(6, take(6))
    move("half+", 0, isend, 6, ihalf, 1, up)
    move("half-", 1, isend, 6, ihalf, 1, down)
    score(4, 2, EARLY, TEXTS)
    image_grad(4, 2)
    put(4, take(4, half, half), half)
    put(5, take(5, 0, half))
    move("pfull+1", 1, isend, 4, ifull, 0, up)
    move("pfull-0", 0, isend, 5, ifull, 1, down)
    score(0, 4, EARLY, TEXTS)

    def grad_rows(slot):
        return tgrad[slot * rows : (slot + 1) * rows]

    def put_text(n, value):
        tsend[n * rows : (n + 1) * rows] = value.astype(jnp.bfloat16)

    def got_text(n):
        return trecv[n * rows : (n + 1) * rows].astype(jnp.float32)

    text_grad(EARLY, TEXTS)
    put_text(6, grad_rows(6))
    send("gfar", block(tsend, 6), block(trecv, 5), far)
    put_text(5, grad_rows(5))
    send("gsib2", block(tsend, 5), block(trecv, 2), sibling)

    def got_half(n, start):
        begin = n * rows + start
        return ihalf[begin : begin + half].astype(jnp.float32)

    arrived("phalf+", "phalf-")
    put(4, take(4, 0, half) + got_half(0, 0))
    put(5, take(5, half, half) + got_half(0, half), half)
    move("pfull+0", 0, isend, 4, ifull, 0, up)
    move("pfull-1", 1, isend, 5, ifull, 1, down)

    image_grad(0, 4)
    put(2, take(2, half, half), half)
    put(3, take(3, 0, half))
    move("full+1", 1, isend, 2, ifull, 2, up)
    move("full-0", 0, isend, 3, ifull, 3, down)

    text_grad(0, EARLY)
    put_text(3, grad_rows(3))
    send("gsib1", block(tsend, 3), block(trecv, 1), sibling)
    put_text(1, grad_rows(1))
    send("gsib", block(tsend, 1), block(trecv, 0), sibling)

    arrived("half+", "half-")
    put(2, take(2, 0, half) + got_half(1, 0))
    put(3, take(3, half, half) + got_half(1, half), half)
    move("full+0", 0, isend, 2, ifull, 2, up)
    move("full-1", 1, isend, 3, ifull, 3, down)

    arrived("gsib2")

    def send_second(extra):
        put_text(4, grad_rows(4) + got_text(2) + extra)
        send("gsecond", block(tsend, 4), block(trecv, 3 + at_second), second, at_second - 1)

    def send_first(extra):
        put_text(2, grad_rows(2) + got_text(1) + extra)
        send("gfirst", block(tsend, 2), block(trecv, 3 + at_first), first, at_first)

    arrived("gsib1", "gfar")
    send_second(jnp.where(by_first, 0.0, got_text(5)))
    send_first(jnp.where(by_first, got_text(5), 0.0))

    def got_full(n):
        return ifull[n * rows : (n + 1) * rows].astype(jnp.float32)

    arrived("pfull+0", "pfull+1", "pfull-0", "pfull-1")
    put(1, take(1) + got_full(0) + got_full(1))
    send("xsum", block(isend, 1), block(ifull, 4), x_dev)

    arrived("gsib")
    came("gfirst", block(trecv, 3))
    came("gsecond", block(trecv, 4))
    def back(ref, grad):
        unit, inverse = unit_of(ref)
        return inverse * (grad - unit * jnp.sum(unit * grad, axis=-1, keepdims=True))

    cap_hat_grad = grad_rows(0) + got_text(0) + got_text(3) + got_text(4)
    cap_out[...] = back(cap, cap_hat_grad)

    arrived("full+0", "full+1", "full-0", "full-1", "xsum")
    pic_out[...] = back(pic, take(0) + got_full(2) + got_full(3) + got_full(4))

    for name in COPIES:
        copies[name].wait_send()


def shards(picture_embedding_raw, caption_embedding_raw, score_sharpness, score_shift_term):
    rows, width = picture_embedding_raw.shape
    n_pool = lax.axis_size("pool")
    result = jax.ShapeDtypeStruct((rows, width), jnp.float32)

    def blocks(count, dtype=jnp.bfloat16):
        return pltpu.VMEM((count * rows, width), dtype)

    vmem = pl.BlockSpec(memory_space=pltpu.VMEM)
    smem = pl.BlockSpec(memory_space=pltpu.SMEM)
    hbm = pl.BlockSpec(memory_space=pltpu.HBM)
    return pl.pallas_call(
        kernel,
        out_shape=(result, result),
        in_specs=[smem, smem, hbm, hbm],
        out_specs=(vmem, vmem),
        scratch_shapes=[
            blocks(1),
            blocks(1),
            blocks(n_pool),
            blocks(TEXTS),
            pltpu.VMEM((n_pool * rows, TEXTS * rows), jnp.bfloat16),
            blocks(n_pool, jnp.float32),
            blocks(TEXTS, jnp.float32),
            blocks(n_pool),
            blocks(2),
            blocks(5),
            blocks(TEXTS),
            blocks(6),
            pltpu.SemaphoreType.DMA((len(COPIES),)),
            pltpu.SemaphoreType.DMA((len(COPIES),)),
            pltpu.SemaphoreType.DMA((2,)),
        ],
        compiler_params=pltpu.CompilerParams(
            collective_id=0, has_side_effects=True, vmem_limit_bytes=40 * 2**20
        ),
    )(score_sharpness, score_shift_term, picture_embedding_raw, caption_embedding_raw)

def solution(mesh):
    return jax.shard_map(
        shards,
        mesh=mesh,
        in_specs=(P(("loop", "pool"), None), P(("loop", "pool"), None), P(), P()),
        out_specs=(P(("loop", "pool"), None), P(("loop", "pool"), None)),
        check_vma=False,
    )
```

time: 75.8 us -> 65.2 us (0.86)
  the two profiles are of different devices: /device:TPU:6 before, /device:TPU:1 now
where the time goes in v2:
time: 65.2 us; the launch traced here: 65 us
  Pallas kernels  59.5 us (91%)
  local copies, waits for them, and re-layouts  3.55 us (5%)
  between operations  1.94 us (3%)
    pallas_call x1, Pallas kernels, shards(): pl.pallas_call(kernel, out_shape=(result, result), in_specs=[smem, smem,...  59.5 us
    unnamed x6, local copies, waits for them, and re-layouts  3.55 us

profile of v2, /device:TPU:1, one launch (start us, length us, event | category | flops | bytes accessed | tf_op | source)
XLA Modules:
  0.0 65.0 jit_solution(14828220590358907550)
XLA Ops:
  1.9 0.0 copy-start
  1.9 1.0 %copy-done = bf16[128,1152]{1,0:T(8,128)(2,1)S(1)} copy-done((bf16[128,1152]{1,0:T(8,128)(2,1)S(1)}, bf16[128,1152]{1,0:T(8,128)(2,1)}, u32[]{:S(2)}) %copy-start) | copy-done | bytes 294936
  2.9 0.0 copy-start.1
  2.9 1.0 %copy-done.1 = bf16[128,1152]{1,0:T(8,128)(2,1)S(1)} copy-done((bf16[128,1152]{1,0:T(8,128)(2,1)S(1)}, bf16[128,1152]{1,0:T(8,128)(2,1)}, u32[]{:S(2)}) %copy-start.1) | copy-done | bytes 294936
  3.8 59.5 %shard_map.59 = (f32[128,1152]{1,0:T(8,128)S(1)}, f32[128,1152]{1,0:T(8,128)S(1)}) custom-call(f32[1]{0:T(128)S(6)} %copy.8.sharp_ref, f32[1]{0:T(128)S(6)} %copy.9.shift_ref, bf16[128,1152]{1,0:T(8,128)(2,1)S(1)} %copy-done, bf16[128,1152]{1,0:T(8,128)(2,1)S(1)} %copy-done.1), custom_call_target="tpu_custom_call" | custom-call | tf_op jit(solution)/shard_map/pallas_call | solution.py:356
  63.4 0.8 %copy.10 = f32[128,1152]{1,0:T(8,128)} copy(f32[128,1152]{1,0:T(8,128)S(1)} %get-tuple-element.4) | data formatting | bytes 1179648
  64.2 0.8 %copy.11 = f32[128,1152]{1,0:T(8,128)} copy(f32[128,1152]{1,0:T(8,128)S(1)} %get-tuple-element.5) | data formatting | bytes 1179648
Async XLA Ops:
  1.9 1.0 %copy-start = (bf16[128,1152]{1,0:T(8,128)(2,1)S(1)}, bf16[128,1152]{1,0:T(8,128)(2,1)}, u32[]{:S(2)}) copy-start(bf16[128,1152]{1,0:T(8,128)(2,1)} %pic_ref.1) | copy-start | bytes 884740
  2.9 1.0 %copy-start.1 = (bf16[128,1152]{1,0:T(8,128)(2,1)S(1)}, bf16[128,1152]{1,0:T(8,128)(2,1)}, u32[]{:S(2)}) copy-start(bf16[128,1152]{1,0:T(8,128)(2,1)} %cap_ref.1) | copy-start | bytes 884740

commit v3 on v2

--- a/solution.py
+++ b/solution.py
@@ -11,12 +11,16 @@
 TEXTS = 7
 EARLY = 4
 
+QUARTERS = 4
+PARTS = {"A": (0, 2), "B": (2, 2), "A0": (0, 1), "A1": (1, 1), "B0": (2, 1), "B1": (3, 1)}
+
 COPIES = (
-    "x0", "x1", "own+0", "own+1", "own-0", "own-1", "part+0", "part+1", "part-0", "part-1",
-    "fwd+", "fwd-", "pfwd+", "pfwd-",
+    "xA", "xB0", "xB2", "xB3", "xB6", "ownA+", "ownA-", "ownB+", "ownB-", "partA+", "partA-",
+    "fwdA+", "fwdA-", "fwdB+", "fwdB-", "pfwdA+", "pfwdA-",
     "tsib", "tfirst", "tsecond", "tfar", "tsib1", "tsib2",
-    "half+", "half-", "phalf+", "phalf-", "pfull+0", "pfull+1", "pfull-0", "pfull-1",
-    "full+0", "full+1", "full-0", "full-1", "xsum",
+    "xsum7", "xsum4", "xsum5", "xsum1", "xsumA", "phalfA+", "phalfA-", "halfA+", "halfA-", "halfB+", "halfB-",
+    "pfullA+0", "pfullA+1", "pfullA-0", "pfullA-1", "fullA+0", "fullA+1", "fullA-0", "fullA-1",
+    "fullB+", "fullB-",
     "gsib", "gsib1", "gsib2", "gfirst", "gsecond", "gfar",
 )
 NUMBER = {name: i for i, name in enumerate(COPIES)}
@@ -34,7 +38,7 @@
 
 def kernel(
     sharp_ref, shift_ref, pic_ref, cap_ref, pic_out, cap_out,
-    pic, cap, img, txt, weights, part, tgrad, isend, ihalf, ifull, tsend, trecv,
+    pic, cap, img, txt, weights, part_sum, tgrad, isend, ixsum, ihalf, ifull, tsend, trecv,
     send_sem, recv_sem, load_sem,
 ):
     rows, width = pic_ref.shape
@@ -44,7 +48,7 @@
     ]
     for load in loads:
         load.start()
-    half = rows // 2
+    quarter = rows // QUARTERS
     n_loop = lax.axis_size("loop")
     n_z = n_loop // 4
     group, cls = lax.axis_index("loop"), lax.axis_index("pool")
@@ -133,15 +137,19 @@
     pl.semaphore_wait(barrier, jnp.where(low, 7 - beyond, 7))
     greet_across()
 
-    def half_of(ref, slot, n):
-        return block(ref, slot, n * half, half)
-
-    def move(name, n, ref, slot, dst, dst_slot, device):
-        send(name, half_of(ref, slot, n), half_of(dst, dst_slot, n), device)
-
-    move("x0", 0, img, 0, img, 1, x_dev)
-    move("own+0", 0, img, 0, img, 3, up)
-    move("own-1", 1, img, 0, img, 2, down)
+    def place(part):
+        first_quarter, count = PARTS[part]
+        return first_quarter * quarter, count * quarter
+
+    def piece(ref, slot, part):
+        return block(ref, slot, *place(part))
+
+    def move(name, part, ref, slot, dst, dst_slot, device):
+        send(name, piece(ref, slot, part), piece(dst, dst_slot, part), device)
+
+    move("xA", "A", img, 0, img, 1, x_dev)
+    move("ownB+", "B", img, 0, img, 3, up)
+    move("ownB-", "B", img, 0, img, 2, down)
     send("tsib", block(txt, 0), block(txt, 1), sibling)
     make("tsecond", block(txt, 0), block(txt, 2 + 2 * at_second), second, at_second - 1)
     make("tfar", block(txt, jnp.where(by_first, 2, 4)), block(txt, 6), far)
@@ -151,20 +159,21 @@
         copies["tsecond"].start()
 
     send("tfirst", block(txt, 0), block(txt, 2 + 2 * at_first), first, at_first)
-    move("own+1", 1, img, 0, img, 3, up)
-    move("own-0", 0, img, 0, img, 2, down)
-
-    arrived("x0")
-    move("x1", 1, img, 0, img, 1, x_dev)
-    move("part+0", 0, img, 1, img, 5, up)
-    move("part-0", 0, img, 1, img, 4, down)
-    arrived("own+0", "own-1")
-    move("fwd+", 0, img, 3, img, 6, up)
-    move("fwd-", 1, img, 2, img, 6, down)
-
-    arrived("x1")
-    move("part-1", 1, img, 1, img, 4, down)
-    move("part+1", 1, img, 1, img, 5, up)
+    move("ownA+", "A", img, 0, img, 3, up)
+    move("ownA-", "A", img, 0, img, 2, down)
+    move("xB0", "B", img, 0, img, 1, x_dev)
+
+    arrived("ownB+", "ownB-")
+    move("fwdB+", "B0", img, 3, img, 6, up)
+    move("fwdB-", "B1", img, 2, img, 6, down)
+    move("xB2", "B", img, 2, img, 4, x_dev)
+    move("xB3", "B", img, 3, img, 5, x_dev)
+    arrived("xA")
+    move("partA+", "A", img, 1, img, 5, up)
+    move("partA-", "A", img, 1, img, 4, down)
+    arrived("ownA+", "ownA-")
+    move("fwdA+", "A0", img, 3, img, 6, up)
+    move("fwdA-", "A1", img, 2, img, 6, down)
     came("tfirst", block(txt, 2))
     send("tsib1", block(txt, 2), block(txt, 3), sibling)
 
@@ -172,6 +181,8 @@
     def _():
         copies["tfar"].start()
 
+    arrived("fwdB+", "fwdB-")
+    move("xB6", "B", img, 6, img, 7, x_dev)
     make("tsib2", block(txt, 4), block(txt, 5), sibling)
 
     def second_text():
@@ -186,7 +197,7 @@
     def _():
         second_text()
 
-    arrived("own+1", "own-0", "tsib", "tsib1")
+    arrived("xB0", "tsib", "tsib1")
 
     def score(slot, count, begin, end):
         here = pl.ds(slot * rows, count * rows)
@@ -203,7 +214,7 @@
 
     def image_grad(slot, count):
         here = pl.ds(slot * rows, count * rows)
-        part[here] = jnp.dot(weights[here], txt[...], preferred_element_type=jnp.float32)
+        part_sum[here] = jnp.dot(weights[here], txt[...], preferred_element_type=jnp.float32)
 
     def text_grad(begin, end):
         tgrad[begin * rows : end * rows] = lax.dot_general(
@@ -211,19 +222,24 @@
             preferred_element_type=jnp.float32,
         )
 
-    def take(slot, start=0, size=rows):
-        return part[slot * rows + start : slot * rows + start + size]
-
-    def put(slot, value, start=0):
-        begin = slot * rows + start
-        isend[begin : begin + value.shape[0]] = value.astype(jnp.bfloat16)
+    def take(slot, part):
+        start, size = place(part)
+        return part_rows(part_sum, slot, start, size)
+
+    def part_rows(ref, slot, start, size):
+        return ref[slot * rows + start : slot * rows + start + size]
+
+    def put(slot, part, *extra):
+        start, size = place(part)
+        value = take(slot, part)
+        for ref, ref_slot in extra:
+            value = value + part_rows(ref, ref_slot, start, size).astype(jnp.float32)
+        isend[slot * rows + start : slot * rows + start + size] = value.astype(jnp.bfloat16)
 
     score(0, 4, 0, EARLY)
-    arrived("part+0", "part-1")
-    move("pfwd+", 0, img, 5, img, 7, up)
-    move("pfwd-", 1, img, 4, img, 7, down)
-    arrived("part+1", "part-0")
-    score(4, 2, 0, EARLY)
+    arrived("partA+", "partA-")
+    move("pfwdA+", "A0", img, 5, img, 7, up)
+    move("pfwdA-", "A1", img, 4, img, 7, down)
 
     @pl.when(low & (beyond > 0))
     def _():
@@ -237,29 +253,42 @@
         def _():
             copies["tfar"].start()
 
+    arrived("xB2", "xB3")
+    score(4, 2, 0, EARLY)
+
     @pl.when(across)
     def _():
         second_text()
 
-    arrived("fwd+", "fwd-", "pfwd+", "pfwd-")
+    arrived("fwdA+", "fwdA-", "pfwdA+", "pfwdA-", "xB6")
     score(6, 2, 0, EARLY)
 
     arrived("tsib2", "tfar")
     score(6, 2, EARLY, TEXTS)
     image_grad(6, 2)
-    put(7, take(7))
-    move("phalf+", 0, isend, 7, ihalf, 0, up)
-    move("phalf-", 1, isend, 7, ihalf, 0, down)
-    put(6, take(6))
-    move("half+", 0, isend, 6, ihalf, 1, up)
-    move("half-", 1, isend, 6, ihalf, 1, down)
+    put(7, "B")
+    move("xsum7", "B", isend, 7, ixsum, 3, x_dev)
+    put(7, "A")
+    move("phalfA+", "A0", isend, 7, ihalf, 0, up)
+    move("phalfA-", "A1", isend, 7, ihalf, 0, down)
+    put(6, "A")
+    move("halfA+", "A0", isend, 6, ihalf, 1, up)
+    move("halfA-", "A1", isend, 6, ihalf, 1, down)
     score(4, 2, EARLY, TEXTS)
     image_grad(4, 2)
-    put(4, take(4, half, half), half)
-    put(5, take(5, 0, half))
-    move("pfull+1", 1, isend, 4, ifull, 0, up)
-    move("pfull-0", 0, isend, 5, ifull, 1, down)
+    put(4, "B")
+    move("xsum4", "B", isend, 4, ixsum, 1, x_dev)
+    put(5, "B")
+    move("xsum5", "B", isend, 5, ixsum, 2, x_dev)
+    put(4, "A1")
+    move("pfullA+1", "A1", isend, 4, ifull, 0, up)
+    put(5, "A0")
+    move("pfullA-0", "A0", isend, 5, ifull, 1, down)
     score(0, 4, EARLY, TEXTS)
+    arrived("xsum7")
+    put(6, "B", (ixsum, 3))
+    move("halfB+", "B0", isend, 6, ihalf, 1, up)
+    move("halfB-", "B1", isend, 6, ihalf, 1, down)
 
     def grad_rows(slot):
         return tgrad[slot * rows : (slot + 1) * rows]
@@ -276,21 +305,25 @@
     put_text(5, grad_rows(5))
     send("gsib2", block(tsend, 5), block(trecv, 2), sibling)
 
-    def got_half(n, start):
-        begin = n * rows + start
-        return ihalf[begin : begin + half].astype(jnp.float32)
-
-    arrived("phalf+", "phalf-")
-    put(4, take(4, 0, half) + got_half(0, 0))
-    put(5, take(5, half, half) + got_half(0, half), half)
-    move("pfull+0", 0, isend, 4, ifull, 0, up)
-    move("pfull-1", 1, isend, 5, ifull, 1, down)
+    arrived("phalfA+", "phalfA-")
+    put(4, "A0", (ihalf, 0))
+    move("pfullA+0", "A0", isend, 4, ifull, 0, up)
+    put(5, "A1", (ihalf, 0))
+    move("pfullA-1", "A1", isend, 5, ifull, 1, down)
 
     image_grad(0, 4)
-    put(2, take(2, half, half), half)
-    put(3, take(3, 0, half))
-    move("full+1", 1, isend, 2, ifull, 2, up)
-    move("full-0", 0, isend, 3, ifull, 3, down)
+    put(1, "B")
+    move("xsum1", "B", isend, 1, ixsum, 0, x_dev)
+    put(2, "A1")
+    move("fullA+1", "A1", isend, 2, ifull, 2, up)
+    put(3, "A0")
+    move("fullA-0", "A0", isend, 3, ifull, 3, down)
+
+    arrived("halfA+", "halfA-")
+    put(2, "A0", (ihalf, 1))
+    move("fullA+0", "A0", isend, 2, ifull, 2, up)
+    put(3, "A1", (ihalf, 1))
+    move("fullA-1", "A1", isend, 3, ifull, 3, down)
 
     text_grad(0, EARLY)
     put_text(3, grad_rows(3))
@@ -298,32 +331,38 @@
     put_text(1, grad_rows(1))
     send("gsib", block(tsend, 1), block(trecv, 0), sibling)
 
-    arrived("half+", "half-")
-    put(2, take(2, 0, half) + got_half(1, 0))
-    put(3, take(3, half, half) + got_half(1, half), half)
-    move("full+0", 0, isend, 2, ifull, 2, up)
-    move("full-1", 1, isend, 3, ifull, 3, down)
-
-    arrived("gsib2")
-
-    def send_second(extra):
-        put_text(4, grad_rows(4) + got_text(2) + extra)
-        send("gsecond", block(tsend, 4), block(trecv, 3 + at_second), second, at_second - 1)
-
-    def send_first(extra):
-        put_text(2, grad_rows(2) + got_text(1) + extra)
-        send("gfirst", block(tsend, 2), block(trecv, 3 + at_first), first, at_first)
-
-    arrived("gsib1", "gfar")
-    send_second(jnp.where(by_first, 0.0, got_text(5)))
-    send_first(jnp.where(by_first, got_text(5), 0.0))
+    arrived("pfullA+0", "pfullA+1", "pfullA-0", "pfullA-1")
+    put(1, "A", (ifull, 0), (ifull, 1))
+    move("xsumA", "A", isend, 1, ifull, 4, x_dev)
+
+    arrived("xsum4", "xsum5", "halfB+", "halfB-")
+    put(2, "B0", (ixsum, 1), (ihalf, 1))
+    put(2, "B1", (ixsum, 1))
+    move("fullB+", "B", isend, 2, ifull, 2, up)
+    put(3, "B0", (ixsum, 2))
+    put(3, "B1", (ixsum, 2), (ihalf, 1))
+    move("fullB-", "B", isend, 3, ifull, 3, down)
+
+    def text_rows(ref, slot):
+        return ref[pl.ds(pl.multiple_of(slot * rows, rows), rows)].astype(jnp.float32)
+
+    def pass_back(name, is_first, *parts):
+        slot = jnp.where(is_first, 2, 4)
+        value = text_rows(tgrad, slot) + text_rows(trecv, jnp.where(is_first, 1, 2))
+        for n in parts:
+            value = value + got_text(n)
+        tsend[pl.ds(pl.multiple_of(slot * rows, rows), rows)] = value.astype(jnp.bfloat16)
+        lands = jnp.where(is_first, at_first, at_second)
+        device = tuple(jnp.where(is_first, a, b) for a, b in zip(first, second))
+        send(name, block(tsend, slot), block(trecv, 3 + lands), device, lands - (name == "gsecond"))
+
+    arrived("gsib1", "gsib2")
+    pass_back("gfirst", jnp.logical_not(by_first))
+    arrived("gfar")
+    pass_back("gsecond", by_first, 5)
 
     def got_full(n):
         return ifull[n * rows : (n + 1) * rows].astype(jnp.float32)
-
-    arrived("pfull+0", "pfull+1", "pfull-0", "pfull-1")
-    put(1, take(1) + got_full(0) + got_full(1))
-    send("xsum", block(isend, 1), block(ifull, 4), x_dev)
 
     arrived("gsib")
     came("gfirst", block(trecv, 3))
@@ -335,8 +374,11 @@
     cap_hat_grad = grad_rows(0) + got_text(0) + got_text(3) + got_text(4)
     cap_out[...] = back(cap, cap_hat_grad)
 
-    arrived("full+0", "full+1", "full-0", "full-1", "xsum")
-    pic_out[...] = back(pic, take(0) + got_full(2) + got_full(3) + got_full(4))
+    arrived("fullA+0", "fullA+1", "fullA-0", "fullA-1", "xsumA", "xsum1", "fullB+", "fullB-")
+    size = place("A")[1]
+    crossed = (got_full(4)[:size], ixsum[size : 2 * size].astype(jnp.float32))
+    pic_hat_grad = part_sum[0:rows] + got_full(2) + got_full(3) + jnp.concatenate(crossed, axis=0)
+    pic_out[...] = back(pic, pic_hat_grad)
 
     for name in COPIES:
         copies[name].wait_send()
@@ -367,6 +409,7 @@
             blocks(n_pool, jnp.float32),
             blocks(TEXTS, jnp.float32),
             blocks(n_pool),
+            blocks(4),
             blocks(2),
             blocks(5),
             blocks(TEXTS),

time: 65.2 us -> 61 us (0.936)
  the two profiles are of different devices: /device:TPU:1 before, /device:TPU:6 now
where the time goes in v3:
time: 61 us; the launch traced here: 60 us
  Pallas kernels  54.5 us (89%)
  local copies, waits for them, and re-layouts  3.55 us (6%)
  between operations  1.94 us (3%)
    pallas_call x1, Pallas kernels, shards(): pl.pallas_call(kernel, out_shape=(result, result), in_specs=[smem, smem,...  54.5 us
    unnamed x6, local copies, waits for them, and re-layouts  3.55 us

profile of v3, /device:TPU:6, one launch (start us, length us, event | category | flops | bytes accessed | tf_op | source)
XLA Modules:
  0.0 60.0 jit_solution(2360424570510974485)
XLA Ops:
  1.9 0.0 copy-start
  1.9 1.0 %copy-done = bf16[128,1152]{1,0:T(8,128)(2,1)S(1)} copy-done((bf16[128,1152]{1,0:T(8,128)(2,1)S(1)}, bf16[128,1152]{1,0:T(8,128)(2,1)}, u32[]{:S(2)}) %copy-start) | copy-done | bytes 294936
  2.9 0.0 copy-start.1
  2.9 1.0 %copy-done.1 = bf16[128,1152]{1,0:T(8,128)(2,1)S(1)} copy-done((bf16[128,1152]{1,0:T(8,128)(2,1)S(1)}, bf16[128,1152]{1,0:T(8,128)(2,1)}, u32[]{:S(2)}) %copy-start.1) | copy-done | bytes 294936
  3.8 54.5 %shard_map.59 = (f32[128,1152]{1,0:T(8,128)S(1)}, f32[128,1152]{1,0:T(8,128)S(1)}) custom-call(f32[1]{0:T(128)S(6)} %copy.8.sharp_ref, f32[1]{0:T(128)S(6)} %copy.9.shift_ref, bf16[128,1152]{1,0:T(8,128)(2,1)S(1)} %copy-done, bf16[128,1152]{1,0:T(8,128)(2,1)S(1)} %copy-done.1), custom_call_target="tpu_custom_call" | custom-call | tf_op jit(solution)/shard_map/pallas_call | solution.py:398
  58.4 0.8 %copy.10 = f32[128,1152]{1,0:T(8,128)} copy(f32[128,1152]{1,0:T(8,128)S(1)} %get-tuple-element.4) | data formatting | bytes 1179648
  59.2 0.8 %copy.11 = f32[128,1152]{1,0:T(8,128)} copy(f32[128,1152]{1,0:T(8,128)S(1)} %get-tuple-element.5) | data formatting | bytes 1179648
Async XLA Ops:
  1.9 1.0 %copy-start = (bf16[128,1152]{1,0:T(8,128)(2,1)S(1)}, bf16[128,1152]{1,0:T(8,128)(2,1)}, u32[]{:S(2)}) copy-start(bf16[128,1152]{1,0:T(8,128)(2,1)} %pic_ref.1) | copy-start | bytes 884740
  2.9 1.0 %copy-start.1 = (bf16[128,1152]{1,0:T(8,128)(2,1)S(1)}, bf16[128,1152]{1,0:T(8,128)(2,1)}, u32[]{:S(2)}) copy-start(bf16[128,1152]{1,0:T(8,128)(2,1)} %cap_ref.1) | copy-start | bytes 884740

commit v4 on v3

--- a/solution.py
+++ b/solution.py
@@ -37,17 +37,11 @@
 
 
 def kernel(
-    sharp_ref, shift_ref, pic_ref, cap_ref, pic_out, cap_out,
-    pic, cap, img, txt, weights, part_sum, tgrad, isend, ixsum, ihalf, ifull, tsend, trecv,
-    send_sem, recv_sem, load_sem,
+    sharp_ref, shift_ref, pic, cap, pic_out, cap_out,
+    img, txt, weights, part_sum, tgrad, isend, ixsum, ihalf, ifull, tsend, trecv,
+    send_sem, recv_sem,
 ):
-    rows, width = pic_ref.shape
-    loads = [
-        pltpu.make_async_copy(ref, dst, load_sem.at[n])
-        for n, (ref, dst) in enumerate(((pic_ref, pic), (cap_ref, cap)))
-    ]
-    for load in loads:
-        load.start()
+    rows, width = pic.shape
     quarter = rows // QUARTERS
     n_loop = lax.axis_size("loop")
     n_z = n_loop // 4
@@ -128,9 +122,7 @@
             device_id=first, device_id_type=MESH,
         ).wait_recv()
 
-    loads[0].wait()
     img[0:rows] = unit_of(pic)[0].astype(jnp.bfloat16)
-    loads[1].wait()
     txt[0:rows] = unit_of(cap)[0].astype(jnp.bfloat16)
     sharp, shift = sharp_ref[0], shift_ref[0]
 
@@ -237,21 +229,22 @@
         isend[slot * rows + start : slot * rows + start + size] = value.astype(jnp.bfloat16)
 
     score(0, 4, 0, EARLY)
+
+    @pl.when(low & (beyond > 0))
+    def _():
+        pl.semaphore_wait(barrier, beyond)
+
+        @pl.when(across)
+        def _():
+            copies["tsecond"].start()
+
+        @pl.when(far_across)
+        def _():
+            copies["tfar"].start()
+
     arrived("partA+", "partA-")
     move("pfwdA+", "A0", img, 5, img, 7, up)
     move("pfwdA-", "A1", img, 4, img, 7, down)
-
-    @pl.when(low & (beyond > 0))
-    def _():
-        pl.semaphore_wait(barrier, beyond)
-
-        @pl.when(across)
-        def _():
-            copies["tsecond"].start()
-
-        @pl.when(far_across)
-        def _():
-            copies["tfar"].start()
 
     arrived("xB2", "xB3")
     score(4, 2, 0, EARLY)
@@ -285,10 +278,6 @@
     put(5, "A0")
     move("pfullA-0", "A0", isend, 5, ifull, 1, down)
     score(0, 4, EARLY, TEXTS)
-    arrived("xsum7")
-    put(6, "B", (ixsum, 3))
-    move("halfB+", "B0", isend, 6, ihalf, 1, up)
-    move("halfB-", "B1", isend, 6, ihalf, 1, down)
 
     def grad_rows(slot):
         return tgrad[slot * rows : (slot + 1) * rows]
@@ -318,22 +307,53 @@
     move("fullA+1", "A1", isend, 2, ifull, 2, up)
     put(3, "A0")
     move("fullA-0", "A0", isend, 3, ifull, 3, down)
-
     arrived("halfA+", "halfA-")
     put(2, "A0", (ihalf, 1))
     move("fullA+0", "A0", isend, 2, ifull, 2, up)
     put(3, "A1", (ihalf, 1))
     move("fullA-1", "A1", isend, 3, ifull, 3, down)
 
+    arrived("xsum7")
+    put(6, "B", (ixsum, 3))
+    move("halfB+", "B0", isend, 6, ihalf, 1, up)
+    move("halfB-", "B1", isend, 6, ihalf, 1, down)
+
     text_grad(0, EARLY)
     put_text(3, grad_rows(3))
     send("gsib1", block(tsend, 3), block(trecv, 1), sibling)
     put_text(1, grad_rows(1))
     send("gsib", block(tsend, 1), block(trecv, 0), sibling)
 
+    def pass_back(name, slot, other, more):
+        @pl.when(more)
+        def _():
+            arrived("gfar")
+            put_text(slot, grad_rows(slot) + got_text(other) + got_text(5))
+
+        @pl.when(jnp.logical_not(more))
+        def _():
+            put_text(slot, grad_rows(slot) + got_text(other))
+
+        copies[name].start()
+
+    make("gfirst", block(tsend, 2), block(trecv, 3 + at_first), first, at_first)
+    make("gsecond", block(tsend, 4), block(trecv, 3 + at_second), second, at_second - 1)
+
+    arrived("gsib2")
+    pass_back("gsecond", 4, 2, jnp.logical_not(by_first))
+
     arrived("pfullA+0", "pfullA+1", "pfullA-0", "pfullA-1")
     put(1, "A", (ifull, 0), (ifull, 1))
     move("xsumA", "A", isend, 1, ifull, 4, x_dev)
+
+    arrived("gsib1")
+
+    def pass_first():
+        pass_back("gfirst", 2, 1, by_first)
+
+    @pl.when(jnp.logical_not(low & far_across))
+    def _():
+        pass_first()
 
     arrived("xsum4", "xsum5", "halfB+", "halfB-")
     put(2, "B0", (ixsum, 1), (ihalf, 1))
@@ -343,23 +363,9 @@
     put(3, "B1", (ixsum, 2), (ihalf, 1))
     move("fullB-", "B", isend, 3, ifull, 3, down)
 
-    def text_rows(ref, slot):
-        return ref[pl.ds(pl.multiple_of(slot * rows, rows), rows)].astype(jnp.float32)
-
-    def pass_back(name, is_first, *parts):
-        slot = jnp.where(is_first, 2, 4)
-        value = text_rows(tgrad, slot) + text_rows(trecv, jnp.where(is_first, 1, 2))
-        for n in parts:
-            value = value + got_text(n)
-        tsend[pl.ds(pl.multiple_of(slot * rows, rows), rows)] = value.astype(jnp.bfloat16)
-        lands = jnp.where(is_first, at_first, at_second)
-        device = tuple(jnp.where(is_first, a, b) for a, b in zip(first, second))
-        send(name, block(tsend, slot), block(trecv, 3 + lands), device, lands - (name == "gsecond"))
-
-    arrived("gsib1", "gsib2")
-    pass_back("gfirst", jnp.logical_not(by_first))
-    arrived("gfar")
-    pass_back("gsecond", by_first, 5)
+    @pl.when(low & far_across)
+    def _():
+        pass_first()
 
     def got_full(n):
         return ifull[n * rows : (n + 1) * rows].astype(jnp.float32)
@@ -394,15 +400,12 @@
 
     vmem = pl.BlockSpec(memory_space=pltpu.VMEM)
     smem = pl.BlockSpec(memory_space=pltpu.SMEM)
-    hbm = pl.BlockSpec(memory_space=pltpu.HBM)
     return pl.pallas_call(
         kernel,
         out_shape=(result, result),
-        in_specs=[smem, smem, hbm, hbm],
+        in_specs=[smem, smem, vmem, vmem],
         out_specs=(vmem, vmem),
         scratch_shapes=[
-            blocks(1),
-            blocks(1),
             blocks(n_pool),
             blocks(TEXTS),
             pltpu.VMEM((n_pool * rows, TEXTS * rows), jnp.bfloat16),
@@ -416,7 +419,6 @@
             blocks(6),
             pltpu.SemaphoreType.DMA((len(COPIES),)),
             pltpu.SemaphoreType.DMA((len(COPIES),)),
-            pltpu.SemaphoreType.DMA((2,)),
         ],
         compiler_params=pltpu.CompilerParams(
             collective_id=0, has_side_effects=True, vmem_limit_bytes=40 * 2**20

time: 61 us -> 57.9 us (0.949)
  Pallas kernels: 54.5 us -> 51.4 us
    pallas_call x1, Pallas kernels: 54.5 us -> 51.4 us  [shards(): pl.pallas_call(kernel, out_shape=(result, result), in_specs=[smem, smem,...]
where the time goes in v4:
time: 57.9 us; the launch traced here: 56.9 us
  Pallas kernels  51.4 us (89%)
  local copies, waits for them, and re-layouts  3.55 us (6%)
  between operations  1.94 us (3%)
    pallas_call x1, Pallas kernels, shards(): pl.pallas_call(kernel, out_shape=(result, result), in_specs=[smem, smem,...  51.4 us
    unnamed x6, local copies, waits for them, and re-layouts  3.55 us

profile of v4, /device:TPU:6, one launch (start us, length us, event | category | flops | bytes accessed | tf_op | source)
XLA Modules:
  0.0 56.9 jit_solution(4735204859518395781)
XLA Ops:
  1.9 0.0 copy-start
  1.9 1.0 %copy-done = bf16[128,1152]{1,0:T(8,128)(2,1)S(1)} copy-done((bf16[128,1152]{1,0:T(8,128)(2,1)S(1)}, bf16[128,1152]{1,0:T(8,128)(2,1)}, u32[]{:S(2)}) %copy-start) | copy-done | bytes 294936
  2.9 0.0 copy-start.1
  2.9 1.0 %copy-done.1 = bf16[128,1152]{1,0:T(8,128)(2,1)S(1)} copy-done((bf16[128,1152]{1,0:T(8,128)(2,1)S(1)}, bf16[128,1152]{1,0:T(8,128)(2,1)}, u32[]{:S(2)}) %copy-start.1) | copy-done | bytes 294936
  3.8 51.4 %shard_map.59 = (f32[128,1152]{1,0:T(8,128)S(1)}, f32[128,1152]{1,0:T(8,128)S(1)}) custom-call(f32[1]{0:T(128)S(6)} %copy.8.sharp_ref, f32[1]{0:T(128)S(6)} %copy.9.shift_ref, bf16[128,1152]{1,0:T(8,128)(2,1)S(1)} %copy-done, bf16[128,1152]{1,0:T(8,128)(2,1)S(1)} %copy-done.1), custom_call_target="tpu_custom_call" | custom-call | tf_op jit(solution)/shard_map/pallas_call | solution.py:403
  55.3 0.8 %copy.10 = f32[128,1152]{1,0:T(8,128)} copy(f32[128,1152]{1,0:T(8,128)S(1)} %get-tuple-element.4) | data formatting | bytes 1179648
  56.1 0.8 %copy.11 = f32[128,1152]{1,0:T(8,128)} copy(f32[128,1152]{1,0:T(8,128)S(1)} %get-tuple-element.5) | data formatting | bytes 1179648
Async XLA Ops:
  1.9 1.0 %copy-start = (bf16[128,1152]{1,0:T(8,128)(2,1)S(1)}, bf16[128,1152]{1,0:T(8,128)(2,1)}, u32[]{:S(2)}) copy-start(bf16[128,1152]{1,0:T(8,128)(2,1)} %pic.1) | copy-start | bytes 884740
  2.9 1.0 %copy-start.1 = (bf16[128,1152]{1,0:T(8,128)(2,1)S(1)}, bf16[128,1152]{1,0:T(8,128)(2,1)}, u32[]{:S(2)}) copy-start(bf16[128,1152]{1,0:T(8,128)(2,1)} %cap.1) | copy-start | bytes 884740

commit v5 on v4

--- a/solution.py
+++ b/solution.py
@@ -9,7 +9,7 @@
 epsilon_norm = 1e-06
 
 TEXTS = 7
-EARLY = 4
+EARLY, FAR = 4, 6
 
 QUARTERS = 4
 PARTS = {"A": (0, 2), "B": (2, 2), "A0": (0, 1), "A1": (1, 1), "B0": (2, 1), "B1": (3, 1)}
@@ -253,11 +253,13 @@
     def _():
         second_text()
 
+    arrived("tsib2")
+    score(0, 4, EARLY, FAR)
+    score(4, 2, EARLY, FAR)
     arrived("fwdA+", "fwdA-", "pfwdA+", "pfwdA-", "xB6")
-    score(6, 2, 0, EARLY)
-
-    arrived("tsib2", "tfar")
-    score(6, 2, EARLY, TEXTS)
+    score(6, 2, 0, FAR)
+    arrived("tfar")
+    score(6, 2, FAR, TEXTS)
     image_grad(6, 2)
     put(7, "B")
     move("xsum7", "B", isend, 7, ixsum, 3, x_dev)
@@ -267,7 +269,24 @@
     put(6, "A")
     move("halfA+", "A0", isend, 6, ihalf, 1, up)
     move("halfA-", "A1", isend, 6, ihalf, 1, down)
-    score(4, 2, EARLY, TEXTS)
+
+    def grad_rows(slot):
+        return tgrad[slot * rows : (slot + 1) * rows]
+
+    def put_text(n, value):
+        tsend[n * rows : (n + 1) * rows] = value.astype(jnp.bfloat16)
+
+    def got_text(n):
+        return trecv[n * rows : (n + 1) * rows].astype(jnp.float32)
+
+    score(0, 6, FAR, TEXTS)
+    text_grad(FAR, TEXTS)
+    put_text(6, grad_rows(6))
+    send("gfar", block(tsend, 6), block(trecv, 5), far)
+    text_grad(EARLY, FAR)
+    put_text(5, grad_rows(5))
+    send("gsib2", block(tsend, 5), block(trecv, 2), sibling)
+
     image_grad(4, 2)
     put(4, "B")
     move("xsum4", "B", isend, 4, ixsum, 1, x_dev)
@@ -277,22 +296,6 @@
     move("pfullA+1", "A1", isend, 4, ifull, 0, up)
     put(5, "A0")
     move("pfullA-0", "A0", isend, 5, ifull, 1, down)
-    score(0, 4, EARLY, TEXTS)
-
-    def grad_rows(slot):
-        return tgrad[slot * rows : (slot + 1) * rows]
-
-    def put_text(n, value):
-        tsend[n * rows : (n + 1) * rows] = value.astype(jnp.bfloat16)
-
-    def got_text(n):
-        return trecv[n * rows : (n + 1) * rows].astype(jnp.float32)
-
-    text_grad(EARLY, TEXTS)
-    put_text(6, grad_rows(6))
-    send("gfar", block(tsend, 6), block(trecv, 5), far)
-    put_text(5, grad_rows(5))
-    send("gsib2", block(tsend, 5), block(trecv, 2), sibling)
 
     arrived("phalfA+", "phalfA-")
     put(4, "A0", (ihalf, 0))
@@ -318,29 +321,29 @@
     move("halfB+", "B0", isend, 6, ihalf, 1, up)
     move("halfB-", "B1", isend, 6, ihalf, 1, down)
 
+    def pass_back(name, slot, other, more):
+        @pl.when(more)
+        def _():
+            arrived("gfar")
+            put_text(slot, grad_rows(slot) + got_text(other) + got_text(5))
+
+        @pl.when(jnp.logical_not(more))
+        def _():
+            put_text(slot, grad_rows(slot) + got_text(other))
+
+        copies[name].start()
+
+    make("gfirst", block(tsend, 2), block(trecv, 3 + at_first), first, at_first)
+    make("gsecond", block(tsend, 4), block(trecv, 3 + at_second), second, at_second - 1)
+
+    arrived("gsib2")
+    pass_back("gsecond", 4, 2, jnp.logical_not(by_first))
+
     text_grad(0, EARLY)
     put_text(3, grad_rows(3))
     send("gsib1", block(tsend, 3), block(trecv, 1), sibling)
     put_text(1, grad_rows(1))
     send("gsib", block(tsend, 1), block(trecv, 0), sibling)
-
-    def pass_back(name, slot, other, more):
-        @pl.when(more)
-        def _():
-            arrived("gfar")
-            put_text(slot, grad_rows(slot) + got_text(other) + got_text(5))
-
-        @pl.when(jnp.logical_not(more))
-        def _():
-            put_text(slot, grad_rows(slot) + got_text(other))
-
-        copies[name].start()
-
-    make("gfirst", block(tsend, 2), block(trecv, 3 + at_first), first, at_first)
-    make("gsecond", block(tsend, 4), block(trecv, 3 + at_second), second, at_second - 1)
-
-    arrived("gsib2")
-    pass_back("gsecond", 4, 2, jnp.logical_not(by_first))
 
     arrived("pfullA+0", "pfullA+1", "pfullA-0", "pfullA-1")
     put(1, "A", (ifull, 0), (ifull, 1))

time: 57.9 us -> 55.9 us (0.965)
  Pallas kernels: 51.4 us -> 49.7 us
    pallas_call x1, Pallas kernels: 51.4 us -> 49.7 us  [shards(): pl.pallas_call(kernel, out_shape=(result, result), in_specs=[smem, smem,...]
where the time goes in v5:
time: 55.9 us; the launch traced here: 55.2 us
  Pallas kernels  49.7 us (89%)
  local copies, waits for them, and re-layouts  3.55 us (6%)
  between operations  1.94 us (3%)
    pallas_call x1, Pallas kernels, shards(): pl.pallas_call(kernel, out_shape=(result, result), in_specs=[smem, smem,...  49.7 us
    unnamed x6, local copies, waits for them, and re-layouts  3.55 us

profile of v5, /device:TPU:6, one launch (start us, length us, event | category | flops | bytes accessed | tf_op | source)
XLA Modules:
  0.0 55.2 jit_solution(3394718097011288242)
XLA Ops:
  1.9 0.0 copy-start
  1.9 1.0 %copy-done = bf16[128,1152]{1,0:T(8,128)(2,1)S(1)} copy-done((bf16[128,1152]{1,0:T(8,128)(2,1)S(1)}, bf16[128,1152]{1,0:T(8,128)(2,1)}, u32[]{:S(2)}) %copy-start) | copy-done | bytes 294936
  2.9 0.0 copy-start.1
  2.9 1.0 %copy-done.1 = bf16[128,1152]{1,0:T(8,128)(2,1)S(1)} copy-done((bf16[128,1152]{1,0:T(8,128)(2,1)S(1)}, bf16[128,1152]{1,0:T(8,128)(2,1)}, u32[]{:S(2)}) %copy-start.1) | copy-done | bytes 294936
  3.8 49.7 %shard_map.59 = (f32[128,1152]{1,0:T(8,128)S(1)}, f32[128,1152]{1,0:T(8,128)S(1)}) custom-call(f32[1]{0:T(128)S(6)} %copy.8.sharp_ref, f32[1]{0:T(128)S(6)} %copy.9.shift_ref, bf16[128,1152]{1,0:T(8,128)(2,1)S(1)} %copy-done, bf16[128,1152]{1,0:T(8,128)(2,1)S(1)} %copy-done.1), custom_call_target="tpu_custom_call" | custom-call | tf_op jit(solution)/shard_map/pallas_call | solution.py:406
  53.6 0.8 %copy.10 = f32[128,1152]{1,0:T(8,128)} copy(f32[128,1152]{1,0:T(8,128)S(1)} %get-tuple-element.4) | data formatting | bytes 1179648
  54.4 0.8 %copy.11 = f32[128,1152]{1,0:T(8,128)} copy(f32[128,1152]{1,0:T(8,128)S(1)} %get-tuple-element.5) | data formatting | bytes 1179648
Async XLA Ops:
  1.9 1.0 %copy-start = (bf16[128,1152]{1,0:T(8,128)(2,1)S(1)}, bf16[128,1152]{1,0:T(8,128)(2,1)}, u32[]{:S(2)}) copy-start(bf16[128,1152]{1,0:T(8,128)(2,1)} %pic.1) | copy-start | bytes 884740
  2.9 1.0 %copy-start.1 = (bf16[128,1152]{1,0:T(8,128)(2,1)S(1)}, bf16[128,1152]{1,0:T(8,128)(2,1)}, u32[]{:S(2)}) copy-start(bf16[128,1152]{1,0:T(8,128)(2,1)} %cap.1) | copy-start | bytes 884740

commit v6 on v5

--- a/solution.py
+++ b/solution.py
@@ -228,28 +228,32 @@
             value = value + part_rows(ref, ref_slot, start, size).astype(jnp.float32)
         isend[slot * rows + start : slot * rows + start + size] = value.astype(jnp.bfloat16)
 
+    @pl.when(low & (beyond > 0))
+    def _():
+        pl.semaphore_wait(barrier, beyond)
+
+        @pl.when(across)
+        def _():
+            copies["tsecond"].start()
+
+        @pl.when(far_across)
+        def _():
+            copies["tfar"].start()
+
     score(0, 4, 0, EARLY)
-
-    @pl.when(low & (beyond > 0))
-    def _():
-        pl.semaphore_wait(barrier, beyond)
-
-        @pl.when(across)
-        def _():
-            copies["tsecond"].start()
-
-        @pl.when(far_across)
-        def _():
-            copies["tfar"].start()
 
     arrived("partA+", "partA-")
     move("pfwdA+", "A0", img, 5, img, 7, up)
     move("pfwdA-", "A1", img, 4, img, 7, down)
 
+    @pl.when(across & jnp.logical_not(low))
+    def _():
+        second_text()
+
     arrived("xB2", "xB3")
     score(4, 2, 0, EARLY)
 
-    @pl.when(across)
+    @pl.when(low & across)
     def _():
         second_text()
 

time: 55.9 us -> 54.3 us (0.971)
  the two profiles are of different devices: /device:TPU:6 before, /device:TPU:8 now
where the time goes in v6:
time: 54.3 us; the launch traced here: 54.1 us
  Pallas kernels  48.6 us (90%)
  local copies, waits for them, and re-layouts  3.55 us (7%)
  between operations  1.94 us (4%)
    pallas_call x1, Pallas kernels, shards(): pl.pallas_call(kernel, out_shape=(result, result), in_specs=[smem, smem,...  48.6 us
    unnamed x6, local copies, waits for them, and re-layouts  3.55 us

profile of v6, /device:TPU:8, one launch (start us, length us, event | category | flops | bytes accessed | tf_op | source)
XLA Modules:
  0.0 54.1 jit_solution(14141417437036344555)
XLA Ops:
  1.9 0.0 copy-start
  1.9 1.0 %copy-done = bf16[128,1152]{1,0:T(8,128)(2,1)S(1)} copy-done((bf16[128,1152]{1,0:T(8,128)(2,1)S(1)}, bf16[128,1152]{1,0:T(8,128)(2,1)}, u32[]{:S(2)}) %copy-start) | copy-done | bytes 294936
  2.9 0.0 copy-start.1
  2.9 1.0 %copy-done.1 = bf16[128,1152]{1,0:T(8,128)(2,1)S(1)} copy-done((bf16[128,1152]{1,0:T(8,128)(2,1)S(1)}, bf16[128,1152]{1,0:T(8,128)(2,1)}, u32[]{:S(2)}) %copy-start.1) | copy-done | bytes 294936
  3.8 48.6 %shard_map.59 = (f32[128,1152]{1,0:T(8,128)S(1)}, f32[128,1152]{1,0:T(8,128)S(1)}) custom-call(f32[1]{0:T(128)S(6)} %copy.8.sharp_ref, f32[1]{0:T(128)S(6)} %copy.9.shift_ref, bf16[128,1152]{1,0:T(8,128)(2,1)S(1)} %copy-done, bf16[128,1152]{1,0:T(8,128)(2,1)S(1)} %copy-done.1), custom_call_target="tpu_custom_call" | custom-call | tf_op jit(solution)/shard_map/pallas_call | solution.py:410
  52.5 0.8 %copy.10 = f32[128,1152]{1,0:T(8,128)} copy(f32[128,1152]{1,0:T(8,128)S(1)} %get-tuple-element.4) | data formatting | bytes 1179648
  53.3 0.8 %copy.11 = f32[128,1152]{1,0:T(8,128)} copy(f32[128,1152]{1,0:T(8,128)S(1)} %get-tuple-element.5) | data formatting | bytes 1179648
Async XLA Ops:
  1.9 1.0 %copy-start = (bf16[128,1152]{1,0:T(8,128)(2,1)S(1)}, bf16[128,1152]{1,0:T(8,128)(2,1)}, u32[]{:S(2)}) copy-start(bf16[128,1152]{1,0:T(8,128)(2,1)} %pic.1) | copy-start | bytes 884740
  2.9 1.0 %copy-start.1 = (bf16[128,1152]{1,0:T(8,128)(2,1)S(1)}, bf16[128,1152]{1,0:T(8,128)(2,1)}, u32[]{:S(2)}) copy-start(bf16[128,1152]{1,0:T(8,128)(2,1)} %cap.1) | copy-start | bytes 884740

commit v7 on v6

--- a/solution.py
+++ b/solution.py
@@ -378,20 +378,20 @@
         return ifull[n * rows : (n + 1) * rows].astype(jnp.float32)
 
     arrived("gsib")
-    came("gfirst", block(trecv, 3))
-    came("gsecond", block(trecv, 4))
     def back(ref, grad):
         unit, inverse = unit_of(ref)
         return inverse * (grad - unit * jnp.sum(unit * grad, axis=-1, keepdims=True))
-
-    cap_hat_grad = grad_rows(0) + got_text(0) + got_text(3) + got_text(4)
-    cap_out[...] = back(cap, cap_hat_grad)
 
     arrived("fullA+0", "fullA+1", "fullA-0", "fullA-1", "xsumA", "xsum1", "fullB+", "fullB-")
     size = place("A")[1]
     crossed = (got_full(4)[:size], ixsum[size : 2 * size].astype(jnp.float32))
     pic_hat_grad = part_sum[0:rows] + got_full(2) + got_full(3) + jnp.concatenate(crossed, axis=0)
     pic_out[...] = back(pic, pic_hat_grad)
+
+    came("gfirst", block(trecv, 3))
+    tgrad[0:rows] = grad_rows(0) + got_text(0) + got_text(3)
+    came("gsecond", block(trecv, 4))
+    cap_out[...] = back(cap, grad_rows(0) + got_text(4))
 
     for name in COPIES:
         copies[name].wait_send()

time: 54.3 us -> 53.9 us (level)
  no operation moved by 1% of the time
where the time goes in v7:
time: 53.9 us; the launch traced here: 53.7 us
  Pallas kernels  48.2 us (89%)
  local copies, waits for them, and re-layouts  3.55 us (7%)
  between operations  1.94 us (4%)
    pallas_call x1, Pallas kernels, shards(): pl.pallas_call(kernel, out_shape=(result, result), in_specs=[smem, smem,...  48.2 us
    unnamed x6, local copies, waits for them, and re-layouts  3.55 us

profile of v7, /device:TPU:8, one launch (start us, length us, event | category | flops | bytes accessed | tf_op | source)
XLA Modules:
  0.0 53.7 jit_solution(1577646075852970530)
XLA Ops:
  1.9 0.0 copy-start
  1.9 1.0 %copy-done = bf16[128,1152]{1,0:T(8,128)(2,1)S(1)} copy-done((bf16[128,1152]{1,0:T(8,128)(2,1)S(1)}, bf16[128,1152]{1,0:T(8,128)(2,1)}, u32[]{:S(2)}) %copy-start) | copy-done | bytes 294936
  2.9 0.0 copy-start.1
  2.9 1.0 %copy-done.1 = bf16[128,1152]{1,0:T(8,128)(2,1)S(1)} copy-done((bf16[128,1152]{1,0:T(8,128)(2,1)S(1)}, bf16[128,1152]{1,0:T(8,128)(2,1)}, u32[]{:S(2)}) %copy-start.1) | copy-done | bytes 294936
  3.8 48.2 %shard_map.59 = (f32[128,1152]{1,0:T(8,128)S(1)}, f32[128,1152]{1,0:T(8,128)S(1)}) custom-call(f32[1]{0:T(128)S(6)} %copy.8.sharp_ref, f32[1]{0:T(128)S(6)} %copy.9.shift_ref, bf16[128,1152]{1,0:T(8,128)(2,1)S(1)} %copy-done, bf16[128,1152]{1,0:T(8,128)(2,1)S(1)} %copy-done.1), custom_call_target="tpu_custom_call" | custom-call | tf_op jit(solution)/shard_map/pallas_call | solution.py:410
  52.1 0.8 %copy.10 = f32[128,1152]{1,0:T(8,128)} copy(f32[128,1152]{1,0:T(8,128)S(1)} %get-tuple-element.4) | data formatting | bytes 1179648
  52.9 0.8 %copy.11 = f32[128,1152]{1,0:T(8,128)} copy(f32[128,1152]{1,0:T(8,128)S(1)} %get-tuple-element.5) | data formatting | bytes 1179648
Async XLA Ops:
  1.9 1.0 %copy-start = (bf16[128,1152]{1,0:T(8,128)(2,1)S(1)}, bf16[128,1152]{1,0:T(8,128)(2,1)}, u32[]{:S(2)}) copy-start(bf16[128,1152]{1,0:T(8,128)(2,1)} %pic.1) | copy-start | bytes 884740
  2.9 1.0 %copy-start.1 = (bf16[128,1152]{1,0:T(8,128)(2,1)S(1)}, bf16[128,1152]{1,0:T(8,128)(2,1)}, u32[]{:S(2)}) copy-start(bf16[128,1152]{1,0:T(8,128)(2,1)} %cap.1) | copy-start | bytes 884740
